TPU v7x, 32 devices: a whole 2x2x4 slice. The times are simulated.
32 devices in a mesh: obj: 2 (over core), dp: 4 (over y, x), mp: 4 (over z).
Axes of the slice: x: 2, y: 2, z: 4, core: 2. Of those that a mesh axis runs over, the one named last changes fastest.
Arguments:
- layer_input: bfloat16 [8, 768, 2048], P(('obj', 'dp')), may hold values from -6 to 6
- out_grad: bfloat16 [8, 768, 2048], P(('obj', 'dp')), may hold values from -6 to 6
- segment_ids: int32 [8, 768], P(('obj', 'dp')), may hold values from 0 to 2, as said below
- target_flags: int32 [8, 768], P(('obj', 'dp')), may hold values from 0 to 1, as said below
- hidden_units: int32 [4], P('mp'), may hold values from 1 to 2048, as said below
- block_slot: int32 [4, 16], P('mp'), may hold values from 0 to 15, as said below
- weight_blocks: float32 [4, 16, 1024, 1024], P('mp', 'dp'), may hold values from -0.125 to 0.125
- stats_left: float32 [4, 16, 1024, 1024], P('mp', 'dp'), as said below
- stats_right: float32 [4, 16, 1024, 1024], P('mp', 'dp'), as said below
- roots_left: float32 [4, 16, 1024, 1024], P('mp', 'dp'), as said below
- roots_right: float32 [4, 16, 1024, 1024], P('mp', 'dp'), as said below
- norm_params: float32 [4, 2048], replicated
- norm_moments: float32 [4, 2048], replicated, may hold values from 3.8146973e-06 to 1.5258789e-05
Outputs:
- y_out: bfloat16 [8, 768, 2048], P(('obj', 'dp'))
- x_grad: bfloat16 [8, 768, 2048], P(('obj', 'dp'))
- clipped_grads: float32 [4, 16, 1024, 1024], P('mp', 'dp')
- new_weights: float32 [4, 16, 1024, 1024], P('mp', 'dp')
- new_left: float32 [4, 16, 1024, 1024], P('mp', 'dp')
- new_right: float32 [4, 16, 1024, 1024], P('mp', 'dp')
- param_clipped: float32 [4, 2048], replicated
- new_moments: float32 [4, 2048], replicated
- new_params: float32 [4, 2048], replicated
- grad_norm: float32 [], replicated
Inputs may be any that keep to these rules, and one draw needn't show every extreme that they name: `segment_ids`: within a row the ids never fall and every row holds all 3 documents; each document holds 1 to 384 positions, one of each row exactly 384. `target_flags`: in the first 4 rows a 1 marks a masked position; in the other rows the ones of a row form one contiguous span of one or more positions. `hidden_units`: they sum to 5461; one index of mp holds exactly 2048. `block_slot`: for each index of mp a permutation of the block numbers; slot s lies on index s // 4 of dp. `stats_left`: Symmetric, with a positive diagonal. `stats_right`: Symmetric, with a positive diagonal. `roots_left`: Symmetric, with a positive diagonal. `roots_right`: Symmetric, with a positive diagonal.
All inputs are finite; a program needn't handle non-finite values.
Results may differ from a plain program's by a relative error of at most 0.0057.
Values may be sent and summed in bfloat16 or wider, within the bound.
No kernel may reach another device: no remote copies, remote signals or barrier semaphores. Data moves between devices by JAX's collectives and lax.ppermute only.
A program may use at most 640 MiB of HBM per device.

v0:
```python
import math

import jax
import jax.numpy as jnp
from jax import lax
from jax.sharding import PartitionSpec as P

HEADS = 16
HD = 128
HCAP = 2048


deep_alpha = 48.0**0.5
stat_decay = 0.5
block_rate = 0.3
param_rate = 0.1
highest = lax.Precision.HIGHEST


def segment_positions(segment_ids):
    last_axis = segment_ids.ndim - 1
    index = lax.broadcasted_iota(jnp.int32, segment_ids.shape, last_axis)
    earlier = jnp.concatenate([segment_ids[..., :1] - 1, segment_ids[..., :-1]], axis=-1)
    starts = jnp.where(segment_ids != earlier, index, 0)
    return index - lax.cummax(starts, axis=last_axis)


def rotary_tables(positions, head_dim):
    half_dim = head_dim // 2
    steps_float = jnp.arange(half_dim, dtype=jnp.float32)
    frequency = jnp.exp(-steps_float * (2.0 * math.log(10000.0) / head_dim))
    angle = positions.astype(jnp.float32)[..., None] * frequency
    return (jnp.cos(angle), jnp.sin(angle))


def rotate(value, cosine, sine):
    half_dim = value.shape[-1] // 2
    first_half, second_half = (value[..., :half_dim], value[..., half_dim:])
    cos_wide, sin_wide = (cosine[..., None, :], sine[..., None, :])
    return jnp.concatenate(
        [
            first_half * cos_wide - second_half * sin_wide,
            second_half * cos_wide + first_half * sin_wide,
        ],
        axis=-1,
    )


def unrotate(gradient, cosine, sine):
    half_dim = gradient.shape[-1] // 2
    first_half, second_half = (gradient[..., :half_dim], gradient[..., half_dim:])
    cos_wide, sin_wide = (cosine[..., None, :], sine[..., None, :])
    return jnp.concatenate(
        [
            first_half * cos_wide + second_half * sin_wide,
            second_half * cos_wide - first_half * sin_wide,
        ],
        axis=-1,
    )


def allowed_mask(segment_ids, spans):
    seq_length = segment_ids.shape[-1]
    index = jnp.arange(seq_length, dtype=jnp.int32)
    causal = index[:, None] >= index[None, :]
    same_doc = segment_ids[..., :, None] == segment_ids[..., None, :]
    visible = (spans[..., None, :] == 0) | (spans[..., :, None] == 1) & causal
    return same_doc & visible


def layer_norm(value, gain, shift):
    center = value - jnp.mean(value, axis=-1, keepdims=True)
    inverse = lax.rsqrt(jnp.mean(center * center, axis=-1, keepdims=True) + 1e-05)
    normed = center * inverse
    return (normed * gain + shift, normed, inverse)


def norm_backward(grad_out, normed, inverse, gain):
    scaled = grad_out * gain
    first_mean = jnp.mean(scaled, axis=-1, keepdims=True)
    second_mean = jnp.mean(scaled * normed, axis=-1, keepdims=True)
    input_grad = inverse * (scaled - first_mean - normed * second_mean)
    return (input_grad, jnp.sum(grad_out * normed, axis=0), jnp.sum(grad_out, axis=0))


def right_product(left, right):
    return lax.dot_general(
        left, right, (((1,), (1,)), ((), ())), preferred_element_type=jnp.float32
    )


def token_product(left, right):
    return lax.dot_general(
        left, right, (((0,), (0,)), ((), ())), preferred_element_type=jnp.float32
    )


def per_device(
    layer_input,
    out_grad,
    segment_ids,
    target_flags,
    hidden_units,
    block_slot,
    weight_blocks,
    stats_left,
    stats_right,
    roots_left,
    roots_right,
    norm_params,
    norm_moments,
):
    row_count, seq_length, width = layer_input.shape
    token_count = row_count * seq_length
    heads_here = HEADS // lax.axis_size("mp")
    local_width = heads_here * HD
    hidden_cap = HCAP
    block_size = weight_blocks.shape[-1]
    score_scale = HD ** (-0.5)
    own_count = jnp.sum(target_flags.astype(jnp.float32))
    total_count = lax.psum(own_count, ("obj", "dp"))
    group_total = lax.axis_size("obj") * lax.axis_size("dp")
    group_weight = own_count * group_total / total_count
    owned_low = weight_blocks[0].astype(jnp.bfloat16)
    all_slots = lax.all_gather(owned_low, "dp", axis=0, tiled=True)
    slot_order = block_slot[0]
    ordered = jnp.take(all_slots, slot_order, axis=0)
    row_blocks = width // block_size
    col_blocks = ordered.shape[0] // row_blocks
    weight_panel = (
        ordered.reshape(row_blocks, col_blocks, block_size, block_size)
        .transpose(0, 2, 1, 3)
        .reshape(width, col_blocks * block_size)
    )
    gu_start = 4 * local_width
    input_weight = weight_panel[:, : 3 * local_width]
    output_weight = weight_panel[:, 3 * local_width : gu_start]
    gate_up_weight = weight_panel[:, gu_start : gu_start + 2 * hidden_cap]
    down_weight = weight_panel[:, gu_start + 2 * hidden_cap :]
    flat_input = layer_input.reshape(token_count, width)
    qkv = jnp.dot(flat_input, input_weight, preferred_element_type=jnp.float32).reshape(
        row_count, seq_length, 3, heads_here, HD
    )
    positions = segment_positions(segment_ids)
    cosine, sine = rotary_tables(positions, HD)
    query = rotate(qkv[:, :, 0], cosine, sine).astype(jnp.bfloat16)
    keys_rot = rotate(qkv[:, :, 1], cosine, sine).astype(jnp.bfloat16)
    values = qkv[:, :, 2].astype(jnp.bfloat16)
    spans = jnp.where(lax.axis_index("obj") == 1, target_flags, 0)
    visible = allowed_mask(segment_ids, spans)[:, None]
    scores = (
        jnp.einsum("rqhd,rkhd->rhqk", query, keys_rot, preferred_element_type=jnp.float32)
        * score_scale
    )
    scores = jnp.where(visible, scores, -1000000000.0)
    peak = jnp.max(scores, axis=-1, keepdims=True)
    exponent = jnp.exp(scores - peak)
    row_total = jnp.sum(exponent, axis=-1, keepdims=True)
    log_total = peak + jnp.log(row_total)
    probs_low = (exponent / row_total).astype(jnp.bfloat16)
    context = (
        jnp.einsum("rhqk,rkhd->rqhd", probs_low, values, preferred_element_type=jnp.float32)
        .astype(jnp.bfloat16)
        .reshape(token_count, local_width)
    )
    attn_part = right_product(context, output_weight)
    attn = lax.psum(attn_part, "mp")
    resid_one = deep_alpha * flat_input.astype(jnp.float32) + attn
    hidden, normed_one, inverse_one = layer_norm(resid_one, norm_params[0], norm_params[1])
    hidden_low = hidden.astype(jnp.bfloat16)
    gate_up = jnp.dot(hidden_low, gate_up_weight, preferred_element_type=jnp.float32)
    gate_value = gate_up[:, :hidden_cap]
    up_value = gate_up[:, hidden_cap:]
    live = (jnp.arange(hidden_cap, dtype=jnp.int32) < hidden_units[0]).astype(jnp.float32)
    activated, gelu_back = jax.vjp(jax.nn.gelu, gate_value)
    inner = (activated * up_value * live).astype(jnp.bfloat16)
    ffn_part = right_product(inner, down_weight)
    ffn = lax.psum(ffn_part, "mp")
    resid_two = deep_alpha * hidden + ffn
    output, normed_two, inverse_two = layer_norm(resid_two, norm_params[2], norm_params[3])
    y_out = output.astype(jnp.bfloat16).reshape(row_count, seq_length, width)
    grad_y = group_weight * out_grad.reshape(token_count, width).astype(jnp.float32)
    grad_two, gain_two_grad, shift_two_grad = norm_backward(
        grad_y, normed_two, inverse_two, norm_params[2]
    )
    ffn_grad = grad_two.astype(jnp.bfloat16)
    inner_grad = jnp.dot(ffn_grad, down_weight, preferred_element_type=jnp.float32) * live
    (gate_grad,) = gelu_back(inner_grad * up_value)
    up_grad = inner_grad * activated
    gate_up_grad = jnp.concatenate([gate_grad, up_grad], axis=1).astype(jnp.bfloat16)
    hidden_part = right_product(gate_up_grad, gate_up_weight)
    hidden_back = lax.psum(hidden_part, "mp")
    hidden_grad = deep_alpha * grad_two + hidden_back
    grad_one, gain_one_grad, shift_one_grad = norm_backward(
        hidden_grad, normed_one, inverse_one, norm_params[0]
    )
    attn_grad = grad_one.astype(jnp.bfloat16)
    context_grad = jnp.dot(attn_grad, output_weight, preferred_element_type=jnp.float32).astype(
        jnp.bfloat16
    )
    context_grad = context_grad.reshape(row_count, seq_length, heads_here, HD)
    scores = (
        jnp.einsum("rqhd,rkhd->rhqk", query, keys_rot, preferred_element_type=jnp.float32)
        * score_scale
    )
    probs = jnp.exp(jnp.where(visible, scores, -1000000000.0) - log_total)
    prob_grad = jnp.einsum(
        "rqhd,rkhd->rhqk", context_grad, values, preferred_element_type=jnp.float32
    )
    row_dot = jnp.sum(probs * prob_grad, axis=-1, keepdims=True)
    score_grad = (probs * (prob_grad - row_dot)).astype(jnp.bfloat16)
    query_grad = (
        jnp.einsum("rhqk,rkhd->rqhd", score_grad, keys_rot, preferred_element_type=jnp.float32)
        * score_scale
    )
    key_grad = (
        jnp.einsum("rhqk,rqhd->rkhd", score_grad, query, preferred_element_type=jnp.float32)
        * score_scale
    )
    value_grad = jnp.einsum(
        "rhqk,rqhd->rkhd",
        probs.astype(jnp.bfloat16),
        context_grad,
        preferred_element_type=jnp.float32,
    )
    query_grad = unrotate(query_grad, cosine, sine)
    key_grad = unrotate(key_grad, cosine, sine)
    qkv_grad = (
        jnp.stack([query_grad, key_grad, value_grad], axis=2)
        .astype(jnp.bfloat16)
        .reshape(token_count, 3 * local_width)
    )
    input_part = right_product(qkv_grad, input_weight)
    input_back = lax.psum(input_part.astype(jnp.bfloat16), "mp").astype(jnp.float32)
    x_grad = (
        (deep_alpha * grad_one + input_back)
        .astype(jnp.bfloat16)
        .reshape(row_count, seq_length, width)
    )
    panel_grad = jnp.concatenate(
        [
            token_product(flat_input, qkv_grad),
            token_product(attn_grad, context),
            token_product(hidden_low, gate_up_grad),
            token_product(ffn_grad, inner),
        ],
        axis=1,
    )
    block_grad = (
        panel_grad.reshape(row_blocks, block_size, col_blocks, block_size)
        .transpose(0, 2, 1, 3)
        .reshape(-1, block_size, block_size)
    )
    slot_index = jnp.arange(block_grad.shape[0], dtype=jnp.int32)
    inverse_order = jnp.sum(
        jnp.where(slot_order[None, :] == slot_index[:, None], slot_index[None, :], 0), axis=1
    )
    slot_grad = jnp.take(block_grad, inverse_order, axis=0)
    owned = lax.psum_scatter(slot_grad, "dp", scatter_dimension=0, tiled=True)
    owned = lax.psum(owned, "obj")
    norm_grad = lax.psum(
        jnp.stack([gain_one_grad, shift_one_grad, gain_two_grad, shift_two_grad]), ("obj", "dp")
    )
    first_rank = (lax.axis_index("dp") == 0) & (lax.axis_index("mp") == 0)
    local_squares = jnp.sum(owned * owned) + jnp.where(
        first_rank, jnp.sum(norm_grad * norm_grad), 0.0
    )
    grad_norm = jnp.sqrt(lax.psum(local_squares, ("dp", "mp")))
    clip_factor = 1.0 / jnp.maximum(grad_norm, 1.0)
    weight_master = weight_blocks[0]
    weight_energy = jnp.mean(weight_master * weight_master, axis=(1, 2))
    clipped = owned * clip_factor
    left_outer = jnp.einsum("bij,bkj->bik", clipped, clipped, precision=highest)
    right_outer = jnp.einsum("bji,bjk->bik", clipped, clipped, precision=highest)
    shaped = jnp.einsum(
        "bij,bjk->bik",
        jnp.einsum("bij,bjk->bik", roots_left[0], clipped, precision=highest),
        roots_right[0],
        precision=highest,
    )
    shaped_energy = jnp.mean(shaped * shaped, axis=(1, 2))
    trust = jnp.sqrt(weight_energy) / jnp.sqrt(shaped_energy + 1e-06)
    new_weights = weight_master - block_rate * trust[:, None, None] * shaped
    new_left = stat_decay * stats_left[0] + (1.0 - stat_decay) * left_outer
    new_right = stat_decay * stats_right[0] + (1.0 - stat_decay) * right_outer
    param_clipped = norm_grad * clip_factor
    new_moments = 0.5 * norm_moments + 0.5 * param_clipped * param_clipped
    new_params = norm_params - param_rate * param_clipped / (jnp.sqrt(new_moments) + 1e-08)
    return (
        y_out,
        x_grad,
        clipped[None],
        new_weights[None],
        new_left[None],
        new_right[None],
        param_clipped,
        new_moments,
        new_params,
        grad_norm,
    )


def solution(mesh):
    return jax.shard_map(
        per_device,
        mesh=mesh,
        in_specs=(
            P(("obj", "dp"), None, None),
            P(("obj", "dp"), None, None),
            P(("obj", "dp"), None),
            P(("obj", "dp"), None),
            P("mp"),
            P("mp", None),
            P("mp", "dp", None, None),
            P("mp", "dp", None, None),
            P("mp", "dp", None, None),
            P("mp", "dp", None, None),
            P("mp", "dp", None, None),
            P(),
            P(),
        ),
        out_specs=(
            P(("obj", "dp"), None, None),
            P(("obj", "dp"), None, None),
            P("mp", "dp", None, None),
            P("mp", "dp", None, None),
            P("mp", "dp", None, None),
            P("mp", "dp", None, None),
            P(),
            P(),
            P(),
            P(),
        ),
        check_vma=False,
    )
```

profile of v0, /device:TPU:0, one launch (start us, length us, event | category | flops | bytes accessed | tf_op | source)
XLA Modules:
  0.0 2786.6 jit_solution(2216200523920014814)
XLA Ops:
  23.6 292.8 %all-gather.2.cloned.1.call-done = bf16[16,1024,1024]{2,1,0:T(8,128)(2,1)} async-done(((bf16[4,1024,1024]{2,1,0:T(8,128)(2,1)}), bf16[16,1024,1024]{2,1,0:T(8,128)(2,1)}) %all-gather.2.cloned.1.call-update) | async-done | bytes 33554448 | tf_op jit(solution)/shard_map/all_gather | solution.py:125
  316.4 23.2 fusion.107
  388.6 29.6 %copy_select_fusion = bf16[2,8,1024,1024]{3,1,2,0:T(8,128)(2,1)} fusion(bf16[2,8,1024,1024]{3,2,1,0:T(8,128)(2,1)} %bitcast.182, pred[2,8]{1,0:T(4,128)(4,1)S(1)} %compare_and_fusion.1), kind=kLoop, calls=%fused_computation.7 | loop fusion | flops 16777216 | bytes 67108880 | tf_op jit(solution)/shard_map/jit(_take)/select_n | solution.py:127
  418.3 30.9 %copy.155 = bf16[256,8,8,1024]{3,1,2,0:T(8,128)(2,1)} copy(bf16[256,8,8,1024]{3,2,1,0:T(8,128)(2,1)} %bitcast.183) | data formatting | bytes 67108864
  480.8 221.7 %all-reduce.6.cloned.1.call-done = f32[768,2048]{1,0:T(8,128)} async-done(((f32[768,2048]{1,0:T(8,128)}), f32[768,2048]{1,0:T(8,128)}) %all-reduce.6.cloned.1.call-update) | async-done | bytes 6291472 | tf_op jit(solution)/shard_map/psum | solution.py:167
  765.4 203.9 %all-reduce.8.cloned.1.call-done = f32[768,2048]{1,0:T(8,128)} async-done(((f32[768,2048]{1,0:T(8,128)}), f32[768,2048]{1,0:T(8,128)}) %all-reduce.8.cloned.1.call-update) | async-done | bytes 6291472 | tf_op jit(solution)/shard_map/psum | solution.py:178
  1040.0 23.7 fusion.51
  1063.7 181.5 %all-reduce.10.cloned.1.call-done = f32[768,2048]{1,0:T(8,128)} async-done(((f32[768,2048]{1,0:T(8,128)}), f32[768,2048]{1,0:T(8,128)}) %all-reduce.10.cloned.1.call-update) | async-done | bytes 6291472 | tf_op jit(solution)/shard_map/psum | solution.py:192
  1324.8 43.7 %pad_maximum_fusion = f32[2048,8192]{1,0:T(8,128)} fusion(f32[2048,2048]{1,0:T(8,128)} %fusion.69, f32[2048,4096]{1,0:T(8,128)} %fusion.51, f32[2048,512]{1,0:T(8,128)} %fusion.66, f32[2048,1536]{1,0:T(8,128)} %copy.125), kind=kLoop, calls=%fused_computation.4 | loop fusion | flops 50331648 | bytes 134217728 | tf_op jit(solution)/shard_map/concatenate | solution.py:240
  1368.5 74.7 %copy.156 = f32[256,8,8,1024]{3,2,1,0:T(8,128)} copy(f32[256,8,8,1024]{3,1,2,0:T(8,128)} %bitcast.71) | data formatting | bytes 134217728
  1443.2 56.4 %copy.128 = f32[2,1024,8,1024]{3,1,2,0:T(8,128)} copy(f32[2,1024,8,1024]{3,2,1,0:T(8,128)} %bitcast.73) | data formatting | bytes 134217728 | tf_op jit(solution)/shard_map/reshape | solution.py:250
  1499.6 43.6 %fusion.106 = (f32[16,512,1024]{2,1,0:T(8,128)}, f32[16,512,1024]{2,1,0:T(8,128)}) fusion(f32[16,1024,1024]{2,1,0:T(8,128)} %bitcast.47), kind=kLoop, calls=%fused_computation.191 | loop fusion | bytes 134217728 | tf_op jit(solution)/shard_map/jit(_take)/gather | solution.py:258
  1543.2 22.9 gather_fusion.3
  1566.1 31.9 %copy.130 = f32[16,512,1024]{1,2,0:T(8,128)} copy(f32[16,512,1024]{2,1,0:T(8,128)} %gather_fusion.3) | data formatting | bytes 67108864 | tf_op jit(solution)/shard_map/jit(_take)/gather | solution.py:258
  1621.0 31.9 %copy.129 = f32[16,512,1024]{1,2,0:T(8,128)} copy(f32[16,512,1024]{2,1,0:T(8,128)} %gather_fusion.2) | data formatting | bytes 67108864 | tf_op jit(solution)/shard_map/jit(_take)/gather | solution.py:258
  1652.9 44.9 %maximum_select_fusion = f32[16,1024,1024]{1,2,0:T(8,128)} fusion(f32[16,512,1024]{1,2,0:T(8,128)} %copy.130, f32[16,512,1024]{1,2,0:T(8,128)} %copy.129, pred[16]{0:T(512)(128)(4,1)S(1)} %copy-done.33), kind=kLoop, calls=%fused_computation.5 | loop fusion | flops 33554432 | bytes 134217744 | tf_op jit(solution)/shard_map/jit(_take)/select_n | solution.py:258
  1697.9 557.4 %reduce-scatter.2.cloned.1.call-done = f32[4,1024,1024]{1,2,0:T(8,128)} async-done(((f32[16,1024,1024]{1,2,0:T(8,128)}), f32[4,1024,1024]{1,2,0:T(8,128)}) %reduce-scatter.2.cloned.1.call-update) | async-done | bytes 16777232 | tf_op jit(solution)/shard_map/reduce_scatter | solution.py:259
  2277.0 26.1 psum.62
  2328.9 114.1 %all-reduce.12.cloned.1.call-done = bf16[768,2048]{1,0:T(8,128)(2,1)} async-done(((bf16[768,2048]{1,0:T(8,128)(2,1)}), bf16[768,2048]{1,0:T(8,128)(2,1)}) %all-reduce.12.cloned.1.call-update) | async-done | bytes 3145744 | tf_op jit(solution)/shard_map/psum | solution.py:234
  2449.6 40.5 %psum.63 = f32[]{:T(128)} all-reduce(f32[]{:T(128)S(6)} %add.175), channel_id=1, replica_groups=mesh['obj'=2,'dp'=4,'mp'=4] {'dp','mp'}, use_global_device_ids=true, to_apply=%region_29.30 | all-reduce | flops 1 | bytes 8 | tf_op jit(solution)/shard_map/psum | solution.py:268
  2520.3 62.8 %fusion.6 = f32[4,1024,1024]{1,2,0:T(8,128)} fusion(f32[1,4,1024,1024]{3,2,1,0:T(8,128)} %param.22, f32[4,1024,1024]{1,2,0:T(8,128)} %all-reduce.14.cloned.1.call-done, f32[]{:T(128)S(6)} %div.62), kind=kOutput, calls=%fused_computation.16 | convolution fusion | flops 51543801856 | bytes 50331652 | tf_op jit(solution)/shard_map/bij,bjk->bik/dot_general | solution.py:277
  2583.1 60.4 %multiply_reduce_fusion = (f32[4]{0:T(128)S(1)}, f32[4,1024,1024]{2,1,0:T(8,128)}) fusion(f32[4,1024,1024]{1,2,0:T(8,128)} %fusion.6, f32[1,4,1024,1024]{3,2,1,0:T(8,128)} %param.23), kind=kOutput, calls=%fused_computation.23 | convolution fusion | flops 51547996160 | bytes 50331664 | tf_op jit(solution)/shard_map/bij,bjk->bik/dot_general | solution.py:275
  2656.3 61.8 %fusion.3 = f32[1,4,1024,1024]{3,2,1,0:T(8,128)} fusion(f32[1,4,1024,1024]{3,2,1,0:T(8,128)} %param.20, f32[4,1024,1024]{1,2,0:T(8,128)} %all-reduce.14.cloned.1.call-done, f32[]{:T(128)S(6)} %div.62), kind=kOutput, calls=%fused_computation.13 | convolution fusion | flops 51552190464 | bytes 50331652 | tf_op jit(solution)/shard_map/bij,bkj->bik/dot_general | solution.py:273
  2718.1 60.0 %fusion.1 = f32[1,4,1024,1024]{3,2,1,0:T(8,128)} fusion(f32[1,4,1024,1024]{3,2,1,0:T(8,128)} %param.21, f32[4,1024,1024]{1,2,0:T(8,128)} %all-reduce.14.cloned.1.call-done, f32[]{:T(128)S(6)} %div.62), kind=kOutput, calls=%fused_computation.10 | convolution fusion | flops 51552190464 | bytes 50331652 | tf_op jit(solution)/shard_map/bji,bjk->bik/dot_general | solution.py:274
  (195 shorter events, 425.3 us)
Async XLA Ops:
  7.2 309.2 %all-gather.2.cloned.1.call-start = ((), (), s32[]{:S(2)}) async-start(), calls=%async_computation.1 | async-start | bytes 41943040 | tf_op jit(solution)/shard_map/all_gather | solution.py:125
  16.3 686.1 %all-reduce.6.cloned.1.call-start = ((), (), s32[]{:S(2)}) async-start(), calls=%async_computation.2 | async-start | bytes 12582912 | tf_op jit(solution)/shard_map/psum | solution.py:167
  22.2 439.3 %copy-start.12 = (f32[768,64]{1,0:T(8,128)}, f32[768,64]{1,0:T(8,128)S(1)}, u32[]{:S(2)}) copy-start(f32[768,64]{1,0:T(8,128)S(1)} %get-tuple-element.84) | copy-start | bytes 589828
  418.3 30.9 %copy-start.18 = (bf16[1,768,2048]{2,1,0:T(8,128)(2,1)S(1)}, bf16[1,768,2048]{2,1,0:T(8,128)(2,1)}, u32[]{:S(2)}) copy-start(bf16[1,768,2048]{2,1,0:T(8,128)(2,1)} %param.13) | copy-start | bytes 9437188
  479.4 489.9 %all-reduce.8.cloned.1.call-start = ((), (), s32[]{:S(2)}) async-start(), calls=%async_computation.3 | async-start | bytes 12582912 | tf_op jit(solution)/shard_map/psum | solution.py:178
  707.0 21.9 copy-start.1
  747.4 497.8 %all-reduce.10.cloned.1.call-start = ((), (), s32[]{:S(2)}) async-start(), calls=%async_computation.4 | async-start | bytes 12582912 | tf_op jit(solution)/shard_map/psum | solution.py:192
  1023.2 1232.0 %reduce-scatter.2.cloned.1.call-start = ((), (), s32[]{:S(2)}) async-start(), calls=%async_computation.6 | async-start | bytes 83886080 | tf_op jit(solution)/shard_map/reduce_scatter | solution.py:259
  1040.0 205.2 %copy-start.28 = (f32[1,2048]{1,0:T(1,128)S(1)}, f32[1,2048]{1,0:T(1,128)}, u32[]{:S(2)}) copy-start(f32[1,2048]{1,0:T(1,128)} %get-tuple-element.83) | copy-start | bytes 24580
  1275.7 10.4 copy-start.8
  1275.7 10.4 copy-start.10
  1275.7 14.8 copy-start.20
  1621.0 31.9 %copy-start.33 = (pred[16]{0:T(512)(128)(4,1)S(1)}, pred[16]{0:T(512)(128)(4,1)}, u32[]{:S(2)}) copy-start(pred[16]{0:T(512)(128)(4,1)} %compare_and_fusion) | copy-start | bytes 52
  1697.8 619.8 %all-reduce.14.cloned.1.call-start = ((), (), s32[]{:S(2)}) async-start(), calls=%async_computation.7 | async-start | bytes 33554432 | tf_op jit(solution)/shard_map/psum | solution.py:260
  2255.3 187.7 %all-reduce.12.cloned.1.call-start = ((), (), s32[]{:S(2)}) async-start(), calls=%async_computation.5 | async-start | bytes 6291456 | tf_op jit(solution)/shard_map/psum | solution.py:234
  2265.3 11.7 copy-start.25
  2265.3 11.7 copy-start.26
  2265.3 11.7 copy-start.27
  2503.2 16.4 copy-start.24
  2503.2 16.4 copy-start.29
  2520.3 123.1 %slice-start.3 = ((s8[16777216]{0:T(1024)(128)(4,1)}), s8[4194304]{0:T(1024)(128)(4,1)S(1)}, s32[]{:S(2)}) async-start(s8[16777216]{0:T(1024)(128)(4,1)} %bitcast.180), calls=%async_computation.11 | async-start | bytes 8388608
  2520.3 123.1 %slice-start.4 = ((s8[16777216]{0:T(1024)(128)(4,1)}), s8[4194304]{0:T(1024)(128)(4,1)S(1)}, s32[]{:S(2)}) async-start(s8[16777216]{0:T(1024)(128)(4,1)} %bitcast.180), calls=%async_computation.12 | async-start | bytes 8388608
  2583.1 60.4 %slice-start.5 = ((s8[16777216]{0:T(1024)(128)(4,1)}), s8[4194304]{0:T(1024)(128)(4,1)S(1)}, s32[]{:S(2)}) async-start(s8[16777216]{0:T(1024)(128)(4,1)} %bitcast.180), calls=%async_computation.13 | async-start | bytes 8388608
  2583.1 60.4 %slice-start.6 = ((s8[16777216]{0:T(1024)(128)(4,1)}), s8[4194304]{0:T(1024)(128)(4,1)S(1)}, s32[]{:S(2)}) async-start(s8[16777216]{0:T(1024)(128)(4,1)} %bitcast.180), calls=%async_computation.14 | async-start | bytes 8388608
  (28 other events, 121.8 us)
Sparse Core Ops, SparseCore 0:
  16.5 299.9 all-gather.1
  479.5 222.8 all-reduce.5
  747.5 221.7 all-reduce.7
  1023.4 221.7 all-reduce.9
  1697.9 557.2 reduce-scatter.1
  2257.5 59.9 all-reduce.13
  2320.6 122.2 all-reduce.11
where the time goes:
time: 2800 us; the launch traced here: 2790 us
  waiting for transfers between devices  1580 us (56%)
  matrix products  421 us (15%)
  local copies, waits for them, and re-layouts  411 us (15%)
  other arithmetic  267 us (10%)
  blocking collectives  82 us (3%)
    reduce_scatter x1, waiting for transfers between devices, per_device(): owned = lax.psum_scatter(slot_grad, 'dp', scatter_dimension=0, tiled=True)  557 us
    all_gather x1, waiting for transfers between devices, per_device(): all_slots = lax.all_gather(owned_low, 'dp', axis=0, tiled=True)  293 us
    psum x1, waiting for transfers between devices, per_device(): attn = lax.psum(attn_part, 'mp')  222 us
    psum x1, waiting for transfers between devices, per_device(): ffn = lax.psum(ffn_part, 'mp')  204 us
    psum x1, waiting for transfers between devices, per_device(): hidden_back = lax.psum(hidden_part, 'mp')  182 us
    gather x5, local copies, waits for them, and re-layouts, per_device(): slot_grad = jnp.take(block_grad, inverse_order, axis=0)  153 us
    unnamed x96, local copies, waits for them, and re-layouts  133 us
    psum x1, waiting for transfers between devices, per_device(): lax.psum(input_part.astype(jnp.bfloat16), 'mp').astype(jnp.float32)  114 us
  transfers between devices with their start and end apart: 7, of which 7 were waited for; matrix products, arithmetic and copies ran while one was open for 3% of the time, Pallas kernels for 0%

commit v1 on v0

v1 whole, which is shorter than its diff:
```python
import math

import jax
import jax.numpy as jnp
from jax import lax
from jax.experimental import pallas as pl
from jax.experimental.pallas import tpu as pltpu
from jax.sharding import PartitionSpec as P

HEADS = 16
HD = 128
HCAP = 2048
TILE = 512
PAIR = 2 * HD
CHUNK = 192
STRIP = 16

deep_alpha = 48.0**0.5
stat_decay = 0.5
block_rate = 0.3
param_rate = 0.1
F32 = jnp.float32
BF16 = jnp.bfloat16
VMEM_LIMIT = 60 * 1024 * 1024


def dot(left, right):
    return jnp.dot(left, right, preferred_element_type=F32)


def dot_nt(left, right):
    return lax.dot_general(left, right, (((1,), (1,)), ((), ())), preferred_element_type=F32)


def dot_tn(left, right):
    return lax.dot_general(left, right, (((0,), (0,)), ((), ())), preferred_element_type=F32)


def segment_positions(segment_ids):
    last_axis = segment_ids.ndim - 1
    index = lax.broadcasted_iota(jnp.int32, segment_ids.shape, last_axis)
    earlier = jnp.concatenate([segment_ids[..., :1] - 1, segment_ids[..., :-1]], axis=-1)
    starts = jnp.where(segment_ids != earlier, index, 0)
    return index - lax.cummax(starts, axis=last_axis)


def rotary_tables(positions):
    half_dim = HD // 2
    steps_float = jnp.arange(half_dim, dtype=F32)
    frequency = jnp.exp(-steps_float * (2.0 * math.log(10000.0) / HD))
    angle = positions.astype(F32)[:, None] * frequency
    cosine, sine = jnp.cos(angle), jnp.sin(angle)
    cos_wide = jnp.concatenate([cosine, cosine], axis=1)
    sin_wide = jnp.concatenate([-sine, sine], axis=1)
    return jnp.concatenate([cos_wide, cos_wide], axis=1), jnp.concatenate([sin_wide, sin_wide], axis=1)


def swap_halves(value):
    heads = [
        pltpu.roll(value[:, h * HD : (h + 1) * HD], HD // 2, 1) for h in range(value.shape[1] // HD)
    ]
    return jnp.concatenate(heads, axis=1)


def normalize(value):
    center = value - jnp.mean(value, axis=-1, keepdims=True)
    inverse = lax.rsqrt(jnp.mean(center * center, axis=-1, keepdims=True) + 1e-05)
    return center * inverse, inverse


def norm_backward(grad_out, normed, inverse, gain):
    scaled = grad_out * gain
    first_mean = jnp.mean(scaled, axis=-1, keepdims=True)
    second_mean = jnp.mean(scaled * normed, axis=-1, keepdims=True)
    return inverse * (scaled - first_mean - normed * second_mean)


def add_norm_sums(sums, grad_out, normed):
    rows, width = grad_out.shape
    sums[0:8, :] += jnp.sum((grad_out * normed).reshape(rows // 8, 8, width), axis=0)
    sums[8:16, :] += jnp.sum(grad_out.reshape(rows // 8, 8, width), axis=0)


def each_rows(rows, action):
    def step(i, carry):
        action(pl.ds(pl.multiple_of(i * STRIP, STRIP), STRIP))
        return carry

    lax.fori_loop(0, rows // STRIP, step, 0, unroll=4)


def received(inner, total, sent, rows):
    return jnp.where(inner[0] == 1, total[rows, :], sent[rows, :]).astype(F32)


def axis_sum(value, axes):
    for axis in axes:
        size, step = lax.axis_size(axis), 1
        while step < size:
            value = value + lax.ppermute(value, axis, [(i, i ^ step) for i in range(size)])
            step *= 2
    return value


def after(value, *others):
    return lax.optimization_barrier((value, *others))[0]


PAIRS = [(0, 1), (1, 0), (2, 3), (3, 2)]
MIDDLE = [(1, 2), (2, 1)]
CYCLE = 4


def run_slots(parts, computes, inner, before, behind):
    count = len(parts)
    held, totals = list(parts), [None] * count
    paired = middle = None
    done = [parts[-1]]
    for slot in range(count + CYCLE * len(computes) - 1):
        roles = {}
        for k in range(count):
            stage, phase = divmod(slot - k, CYCLE)
            if 0 <= stage < len(computes):
                roles[phase] = (k, stage)
        paired = None if paired is None else after(paired, *done)
        middle = None if middle is None else after(middle, *done)
        started, outgoing, arrived = [], [], paired
        if 2 in roles:
            k = roles[2][0]
            outgoing.append(held[k] + middle)
        if 0 in roles:
            outgoing.append(held[roles[0][0]])
        sending = None
        if outgoing:
            sending = outgoing[0] if len(outgoing) == 1 else jnp.where(inner, *outgoing)
            if paired is not None and len(outgoing) == 1:
                sending = after(sending, paired)
            started.append(sending)
        crossing = None
        if 1 in roles:
            k = roles[1][0]
            crossing = held[k] = held[k] + paired
            started.append(crossing)
        if 2 in roles:
            totals[roles[2][0]] = sending
        middle = None if crossing is None else lax.ppermute(crossing, "mp", MIDDLE)
        paired = None if sending is None else lax.ppermute(sending, "mp", PAIRS)
        done = []
        if slot in before:
            started.append(before[slot](*started, arrived))
        if 3 in roles:
            k, stage = roles[3]
            held[k] = computes[stage](k, totals[k], after(arrived, *started))
            done.append(held[k])
        if slot in behind:
            done.append(behind[slot](*done, *started))
        if not done:
            done = started
        if slot + 2 < count:
            done = [*done, parts[slot + 2]]


class Panel:
    def __init__(self, blocks, order, row_blocks):
        count, block, _ = blocks.shape
        self.order = order
        self.half = block // 2
        self.pieces = blocks.reshape(2 * count, self.half, block)
        self.col_blocks = count // row_blocks
        self.count = 2 * row_blocks

    def piece(self, order, place, col_block):
        return (place // 2 * self.col_blocks + col_block) * 2 + place % 2

    def specs(self, width, col_block, col_part):
        out = []
        for place in range(self.count):

            def index(step, order, place=place):
                return (self.piece(order, place, col_block(step)), 0, col_part(step))

            out.append(pl.BlockSpec((None, self.half, width), index))
        return out


class HiddenPanel:
    def __init__(self, slices, order, row_blocks):
        self.slices = slices
        self.order = order
        self.ranks = slices.shape[0] // 2
        self.rows, self.block = slices.shape[2:]
        self.half = self.ranks * self.rows
        self.col_blocks = slices.shape[1] // row_blocks
        self.count = 2 * row_blocks

    def copy(self, copies, slices, place, col_block, target):
        source = slices.at[pl.ds(place % 2 * self.ranks, self.ranks), place // 2 * self.col_blocks + col_block]
        return copies.start(source, target.at[pl.ds(place * self.ranks, self.ranks)])

    def held(self, number):
        return pltpu.VMEM((number, self.count * self.ranks, self.rows, self.block), BF16)


def whole(shape):
    zeros = (0,) * len(shape)
    return pl.BlockSpec(shape, lambda step, *_: zeros)


def params():
    return pltpu.CompilerParams(vmem_limit_bytes=VMEM_LIMIT)


def cost(micros):
    return pl.CostEstimate(flops=0, bytes_accessed=int(micros * 3.5e6), transcendentals=0)


def project(rows, pieces):
    half = pieces[0].shape[0]
    total = dot(rows[:, :half], pieces[0][...])
    for k in range(1, len(pieces)):
        total = total + dot(rows[:, k * half : (k + 1) * half], pieces[k][...])
    return total


def qkv_forward(panel, tokens, cosine, sine, local_width):
    length, width = tokens.shape
    count, half, block = panel.count, panel.half, panel.pieces.shape[2]

    def body(order, x, cos, sin, w_qk, w_v, q_out, k_out, v_out, acc):
        step = pl.program_id(0)

        @pl.when(step == 0)
        def _():
            acc[:, : 2 * local_width] = dot(x[...], w_qk[...])
            acc[:, 2 * local_width :] = dot(x[...], w_v[...])

        @pl.when(step > 0)
        def _():
            acc[:, : 2 * local_width] += dot(x[...], w_qk[...])
            acc[:, 2 * local_width :] += dot(x[...], w_v[...])

        @pl.when(step == count - 1)
        def _():
            for i, out in enumerate((q_out, k_out)):
                for h in range(local_width // HD):
                    value = acc[:, i * local_width + h * HD : i * local_width + (h + 1) * HD]
                    turned = pltpu.roll(value, HD // 2, 1)
                    out[:, h * HD : (h + 1) * HD] = (value * cos[:, :HD] + turned * sin[:, :HD]).astype(BF16)
            v_out[...] = acc[:, 2 * local_width :].astype(BF16)

    def weight(col_block, size):
        return pl.BlockSpec(
            (None, half, size), lambda s, order: (panel.piece(order, s, col_block), 0, 0)
        )

    return pl.pallas_call(
        body,
        grid_spec=pltpu.PrefetchScalarGridSpec(
            num_scalar_prefetch=1,
            grid=(count,),
            in_specs=[
                pl.BlockSpec((length, half), lambda s, order: (0, s)),
                whole((length, PAIR)),
                whole((length, PAIR)),
                weight(0, block),
                weight(1, local_width),
            ],
            out_specs=[whole((length, local_width))] * 3,
            scratch_shapes=[pltpu.VMEM((length, 3 * local_width), F32)],
        ),
        out_shape=[jax.ShapeDtypeStruct((length, local_width), BF16)] * 3,
        compiler_params=params(),
        cost_estimate=cost(11),
        name="qkv_forward",
    )(panel.order, tokens, cosine, sine, panel.pieces, panel.pieces)


def attend(panel, chunk, q, k, v, seg_col, seg_row, key_col, col_key):
    length, local_width = q.shape
    pairs = local_width // PAIR
    count, half = panel.count, panel.half
    width = count * half
    scale = HD**-0.5

    def body(order, q_in, k_in, v_in, segc, segr, keyc, colk, *refs):
        wo = refs[:count]
        p_out, c_out, a_out, acc = refs[count:]
        step = pl.program_id(0)

        @pl.when(step == 0)
        def _():
            acc[...] = jnp.zeros_like(acc)

        visible = (segc[...] == segr[...]) & (colk[...] <= keyc[...])
        for h in range(2):
            lanes = slice(h * HD, (h + 1) * HD)
            scores = dot_nt(q_in[:, lanes], k_in[:, lanes]) * scale
            scores = jnp.where(visible, scores, -1000000000.0)
            exponent = jnp.exp(scores - jnp.max(scores, axis=-1, keepdims=True))
            probs = exponent * (1.0 / jnp.sum(exponent, axis=-1, keepdims=True))
            probs = probs.astype(BF16)
            p_out[h] = probs
            c_out[:, lanes] = dot(probs, v_in[:, lanes]).astype(BF16)
        for i in range(count):
            cols = slice(i * half, (i + 1) * half)
            acc[:, cols] += dot_nt(c_out[...], wo[i][...])

        @pl.when(step == pairs - 1)
        def _():
            a_out[...] = acc[...].astype(BF16)

    all_spec = pl.BlockSpec((length, PAIR), lambda s, *_: (0, s))
    column = pl.BlockSpec((CHUNK, 1), lambda s, *_: (chunk, 0))
    return pl.pallas_call(
        body,
        grid_spec=pltpu.PrefetchScalarGridSpec(
            num_scalar_prefetch=1,
            grid=(pairs,),
            in_specs=[
                pl.BlockSpec((CHUNK, PAIR), lambda s, *_: (chunk, s)),
                all_spec,
                all_spec,
                column,
                whole((1, length)),
                column,
                whole((1, length)),
            ]
            + panel.specs(PAIR, lambda s: 1, lambda s: pairs + s),
            out_specs=[
                pl.BlockSpec((2, CHUNK, length), lambda s, *_: (s, 0, 0)),
                pl.BlockSpec((CHUNK, PAIR), lambda s, *_: (0, s)),
                whole((CHUNK, width)),
            ],
            scratch_shapes=[pltpu.VMEM((CHUNK, width), F32)],
        ),
        out_shape=[
            jax.ShapeDtypeStruct((2 * pairs, CHUNK, length), BF16),
            jax.ShapeDtypeStruct((CHUNK, local_width), BF16),
            jax.ShapeDtypeStruct((CHUNK, width), BF16),
        ],
        compiler_params=params(),
        cost_estimate=cost(7),
        name="attend",
    )(panel.order, q, k, v, seg_col, seg_row, key_col, col_key, *[panel.pieces] * count)


def attend_backward(
    panel, chunk, last, inner, state, q, k, v, probs, context, cosine, sine, carried, g1_before
):
    tokens, norm, attn, grad_two, back = state
    length, local_width = q.shape
    width = tokens.shape[1]
    pairs = local_width // PAIR
    count = panel.count
    scale = HD**-0.5
    first = carried is None

    def body(order, flag, x, gains, t1, s1, g2, t3, s3, q_in, k_in, v_in, p_in, c_in, cos, sin, *refs):
        wo = refs[:count]
        refs = refs[count:]
        if not first:
            kg_in, vg_in = refs[:2]
            refs = refs[3:]
        g1_out, low_out, sums, qg_out, kg_out, vg_out, cg, kg = refs
        step = pl.program_id(0)

        @pl.when(step == 0)
        def _():
            sums[...] = jnp.zeros_like(sums)

            def strip(rows):
                resid = deep_alpha * x[rows, :].astype(F32) + received(flag, t1, s1, rows)
                normed, inverse = normalize(resid)
                grad = deep_alpha * g2[rows, :] + received(flag, t3, s3, rows)
                add_norm_sums(sums, grad, normed)
                grad_one = norm_backward(grad, normed, inverse, gains[0:1, :])
                g1_out[rows, :] = grad_one
                low_out[rows, :] = grad_one.astype(BF16)

            each_rows(CHUNK, strip)

        cg[...] = project(low_out[...], wo).astype(BF16)
        for h in range(2):
            lanes = slice(h * HD, (h + 1) * HD)
            cg_rows = cg[:, lanes]
            row_dot = jnp.sum(cg_rows.astype(F32) * c_in[:, lanes].astype(F32), axis=-1, keepdims=True)
            prob_grad = dot_nt(cg_rows, v_in[:, lanes])
            probs_low = p_in[h]
            score_grad = (probs_low.astype(F32) * (prob_grad - row_dot)).astype(BF16)
            raw = dot(score_grad, k_in[:, lanes]) * scale
            own = pl.ds(chunk * CHUNK, CHUNK)
            turned = pltpu.roll(raw, HD // 2, 1)
            qg_out[:, lanes] = (raw * cos[own, lanes] - turned * sin[own, lanes]).astype(BF16)
            key_grad = dot_tn(score_grad, q_in[:, lanes]) * scale
            value_grad = dot_tn(probs_low, cg_rows)
            if not first:
                key_grad = key_grad + kg_in[:, lanes]
                value_grad = value_grad + vg_in[:, lanes]
            vg_out[:, lanes] = value_grad.astype(vg_out.dtype)
            if last:
                kg[:, lanes] = key_grad
            else:
                kg_out[:, lanes] = key_grad
        if last:
            value = kg[...]
            kg_out[...] = (value * cos[...] - swap_halves(value) * sin[...]).astype(BF16)

    head_spec = pl.BlockSpec((length, PAIR), lambda s, *_: (0, s))
    own_head = pl.BlockSpec((CHUNK, PAIR), lambda s, *_: (0, s))
    rows_spec = whole((CHUNK, width))
    kind = BF16 if last else F32
    in_specs = [pl.BlockSpec((CHUNK, width), lambda s, *_: (chunk, 0)), whole((4, width))]
    in_specs += [rows_spec] * 5
    in_specs += [pl.BlockSpec((CHUNK, PAIR), lambda s, *_: (chunk, s)), head_spec, head_spec]
    in_specs += [pl.BlockSpec((2, CHUNK, length), lambda s, *_: (s, 0, 0)), own_head]
    in_specs += [whole((length, PAIR))] * 2
    in_specs += with_scalars(panel.specs(PAIR, lambda s: 1, lambda s: pairs + s))
    operands = [tokens, norm, *attn, grad_two, *back, q, k, v, probs, context, cosine, sine]
    operands += [panel.pieces] * count
    if not first:
        in_specs += [head_spec] * 2 + any_specs(1)
        operands += [*carried, g1_before]
    g1, low_grad, sums, qg, kg, vg = pl.pallas_call(
        body,
        grid_spec=pltpu.PrefetchScalarGridSpec(
            num_scalar_prefetch=2,
            grid=(pairs,),
            in_specs=in_specs,
            out_specs=[
                pl.BlockSpec((CHUNK, width), lambda s, *_: (chunk, 0)),
                rows_spec,
                whole((16, width)),
                own_head,
                head_spec,
                head_spec,
            ],
            scratch_shapes=[pltpu.VMEM((CHUNK, PAIR), BF16), pltpu.VMEM((length, PAIR), F32)],
        ),
        out_shape=[
            jax.ShapeDtypeStruct((length, width), F32),
            jax.ShapeDtypeStruct((CHUNK, width), BF16),
            jax.ShapeDtypeStruct((16, width), F32),
            jax.ShapeDtypeStruct((CHUNK, local_width), BF16),
            jax.ShapeDtypeStruct((length, local_width), kind),
            jax.ShapeDtypeStruct((length, local_width), kind),
        ],
        input_output_aliases={} if first else {1 + len(operands): 0},
        compiler_params=params(),
        cost_estimate=cost(12),
        name="attend_backward",
    )(panel.order, inner, *operands)
    return g1, low_grad, sums, qg, (kg, vg)


def input_parts(panel, q_grad, k_grad, v_grad):
    chunks = len(q_grad)
    length, local_width = k_grad.shape
    count, half = panel.count, panel.half

    def body(order, *refs):
        qg, kg, vg = refs[:chunks], refs[chunks], refs[chunks + 1]
        wq, wk, wv, out = refs[chunks + 2 :]
        out[...] = (
            dot_nt(stack(qg), wq[...]) + dot_nt(kg[...], wk[...]) + dot_nt(vg[...], wv[...])
        ).astype(BF16)

    def weight(col_block, col_part):
        return pl.BlockSpec(
            (None, half, local_width), lambda s, order: (panel.piece(order, s, col_block), 0, col_part)
        )

    return pl.pallas_call(
        body,
        grid_spec=pltpu.PrefetchScalarGridSpec(
            num_scalar_prefetch=1,
            grid=(count,),
            in_specs=[whole((CHUNK, local_width))] * chunks
            + [whole((length, local_width))] * 2
            + [weight(0, 0), weight(0, 1), weight(1, 0)],
            out_specs=pl.BlockSpec((length, half), lambda s, *_: (0, s)),
        ),
        out_shape=jax.ShapeDtypeStruct((length, count * half), BF16),
        compiler_params=params(),
        cost_estimate=cost(10),
        name="input_parts",
    )(panel.order, *q_grad, k_grad, v_grad, *[panel.pieces] * 3)


def span_of(place, size):
    return pl.ds(pl.multiple_of(place * size, size), size)


def with_scalars(specs):
    return [
        pl.BlockSpec(s.block_shape, lambda step, order, *_, f=s.index_map: f(step, order)) for s in specs
    ]


class Copies:
    def __init__(self, sems):
        self.sems = sems
        self.count = 0

    def start(self, source, target):
        copy = pltpu.make_async_copy(source, target, self.sems.at[self.count])
        copy.start()
        self.count += 1
        return copy


def wait_all(copies):
    for copy in copies:
        copy.wait()


def held_rows(held, place, k, cols):
    per = TILE // held.shape[2]
    return held[place, k * per : (k + 1) * per, :, cols].reshape(TILE, cols.stop - cols.start)


def rising(rows, held, place, cols):
    total = None
    for k in range(rows.shape[1] // TILE):
        product = dot(rows[:, k * TILE : (k + 1) * TILE], held_rows(held, place, k, cols))
        total = product if total is None else total + product
    return total


def falling(acc, value, held, place, cols, first):
    for k in range(acc.shape[1] // TILE):
        span = slice(k * TILE, (k + 1) * TILE)
        product = dot_nt(value, held_rows(held, place, k, cols))
        if first:
            acc[:, span] = product
        else:
            acc[:, span] += product


def any_specs(count):
    return [pl.BlockSpec(memory_space=pl.ANY)] * count


def ffn_forward(panel, chunk, scalars, tokens, norm, total, sent, before):
    width = tokens.shape[1]
    block = panel.block
    span = HCAP // block
    own = pl.ds(chunk * CHUNK, CHUNK)

    def body(order, flags, gains, x_in, t_in, s_in, slices, *refs):
        refs = refs[len(before) :]
        hid_out, low_out, act_out, slope_out, inner_out, f_out = refs[:6]
        x, t1, s1, hid, low, act, slope, inner, f, acc, held, sems = refs[6:]
        copies = Copies(sems)
        rows_in = [copies.start(a, b) for a, b in ((t_in, t1), (s_in, s1), (x_in.at[own], x))]
        weights = {
            (tile, group): [
                panel.copy(copies, slices, k, group * span + tile, held.at[tile * 3 + group])
                for k in range(panel.count)
            ]
            for tile in range(span)
            for group in range(3)
        }
        wait_all(rows_in)

        def norm_strip(rows):
            resid = deep_alpha * x[rows, :].astype(F32) + received(flags, t1, s1, rows)
            normed, _ = normalize(resid)
            value = normed * gains[0:1, :] + gains[1:2, :]
            hid[rows, :] = value
            low[rows, :] = value.astype(BF16)

        each_rows(CHUNK, norm_strip)
        out = [copies.start(hid, hid_out), copies.start(low, low_out.at[own])]
        root = math.sqrt(2.0 / math.pi)
        for tile in range(span):
            wait_all(weights[tile, 0])
            wait_all(weights[tile, 1])
            for part in range(block // TILE):
                cols = slice(part * TILE, (part + 1) * TILE)
                gate = rising(low, held, tile * 3, cols)
                up = rising(low, held, tile * 3 + 1, cols)
                lane = lax.broadcasted_iota(jnp.int32, (1, TILE), 1) + (tile * block + part * TILE)
                live = (lane < flags[1]).astype(F32)
                square = gate * gate
                bend = jnp.tanh(root * gate * (1.0 + 0.044715 * square))
                low_half = 0.5 * (1.0 + bend)
                value = gate * low_half * live
                rise = low_half + 0.5 * gate * (1.0 - bend * bend) * (root * (1.0 + 0.134145 * square))
                act[tile, :, cols] = value.astype(BF16)
                slope[tile, :, cols] = (rise * up * live).astype(BF16)
                inner[tile, :, cols] = (value * up).astype(BF16)
                if part == 0:
                    wait_all(weights[tile, 2])
                falling(acc, inner[tile, :, cols], held, tile * 3 + 2, cols, tile == 0 and part == 0)
            cols = pl.ds(tile * block, block)
            for ref, target in ((act, act_out), (slope, slope_out)):
                out.append(copies.start(ref.at[tile], target.at[:, cols]))
            out.append(copies.start(inner.at[tile], inner_out.at[own, cols]))
        f[...] = acc[...].astype(BF16)
        out.append(copies.start(f, f_out))
        wait_all(out)

    tile_shape = jax.ShapeDtypeStruct((CHUNK, HCAP), BF16)
    low_shape = jax.ShapeDtypeStruct((CHUNK, width), BF16)
    low_rows = pltpu.VMEM((CHUNK, width), BF16)
    wide_rows = pltpu.VMEM((CHUNK, width), F32)
    tiles = pltpu.VMEM((span, CHUNK, block), BF16)
    return pl.pallas_call(
        body,
        grid_spec=pltpu.PrefetchScalarGridSpec(
            num_scalar_prefetch=2,
            grid=(1,),
            in_specs=[whole((4, width))] + any_specs(4 + len(before)),
            out_specs=any_specs(6),
            scratch_shapes=[low_rows] * 3
            + [wide_rows, low_rows]
            + [tiles] * 3
            + [low_rows, wide_rows]
            + [
                panel.held(span * 3),
                pltpu.SemaphoreType.DMA((6 + span * (3 * panel.count + 3),)),
            ],
        ),
        out_shape=[
            jax.ShapeDtypeStruct((CHUNK, width), F32),
            jax.ShapeDtypeStruct(tokens.shape, BF16),
            tile_shape,
            tile_shape,
            jax.ShapeDtypeStruct((tokens.shape[0], HCAP), BF16),
            low_shape,
        ],
        input_output_aliases={7: 1, 8: 4} if before else {},
        compiler_params=params(),
        cost_estimate=cost(14),
        name="ffn_forward",
    )(panel.order, scalars, norm, tokens, total, sent, panel.slices, *before)


def ffn_backward(
    panel, chunk, inner, group_weight, hidden, norm, total, sent, out_grad, act, slope, before
):
    width = hidden.shape[1]
    block = panel.block
    span = HCAP // block
    own = pl.ds(chunk * CHUNK, CHUNK)

    def body(order, flags, scale, gains, hid_in, t_in, s_in, og_in, act_in, slope_in, slices, *refs):
        refs = refs[len(before) :]
        y_out, g2_out, low_out, sums, gate_out, up_out, h_out = refs[:7]
        hid, t2, s2, og, act_rows, slope_rows, y, g2, low, gate, up, h, acc, held, sems = refs[7:]
        copies = Copies(sems)
        pairs = ((t_in, t2), (s_in, s2), (hid_in, hid), (og_in.at[own], og))
        rows_in = [copies.start(a, b) for a, b in pairs]
        saved = [copies.start(act_in, act_rows), copies.start(slope_in, slope_rows)]
        weights = {
            (tile, group): [
                panel.copy(copies, slices, k, group * span + tile, held.at[tile * 3 + group])
                for k in range(panel.count)
            ]
            for tile in range(span)
            for group in (2, 0, 1)
        }
        sums[...] = jnp.zeros_like(sums)
        wait_all(rows_in)

        def norm_strip(rows):
            resid = deep_alpha * hid[rows, :] + received(flags, t2, s2, rows)
            normed, inverse = normalize(resid)
            y[rows, :] = (normed * gains[2:3, :] + gains[3:4, :]).astype(BF16)
            grad = scale[0] * og[rows, :].astype(F32)
            add_norm_sums(sums, grad, normed)
            grad_two = norm_backward(grad, normed, inverse, gains[2:3, :])
            g2[rows, :] = grad_two
            low[rows, :] = grad_two.astype(BF16)

        each_rows(CHUNK, norm_strip)
        out = [copies.start(a, b) for a, b in ((y, y_out.at[own]), (g2, g2_out), (low, low_out.at[own]))]
        wait_all(saved)
        for tile in range(span):
            wait_all(weights[tile, 2])
            for part in range(block // TILE):
                cols = slice(part * TILE, (part + 1) * TILE)
                saved_cols = slice(tile * block + part * TILE, tile * block + (part + 1) * TILE)
                inner_grad = rising(low, held, tile * 3 + 2, cols)
                gate_grad = (inner_grad * slope_rows[:, saved_cols].astype(F32)).astype(BF16)
                up_grad = (inner_grad * act_rows[:, saved_cols].astype(F32)).astype(BF16)
                gate[tile, :, cols] = gate_grad
                up[tile, :, cols] = up_grad
                if part == 0:
                    wait_all(weights[tile, 0])
                    wait_all(weights[tile, 1])
                falling(acc, gate_grad, held, tile * 3, cols, tile == 0 and part == 0)
                falling(acc, up_grad, held, tile * 3 + 1, cols, False)
            cols = pl.ds(tile * block, block)
            for ref, target in ((gate, gate_out), (up, up_out)):
                out.append(copies.start(ref.at[tile], target.at[own, cols]))
        h[...] = acc[...].astype(BF16)
        out.append(copies.start(h, h_out))
        wait_all(out)

    operands = [norm, hidden, total, sent, out_grad, act, slope, panel.slices]
    operands += before
    wide_tile_shape = jax.ShapeDtypeStruct((out_grad.shape[0], HCAP), BF16)
    low_shape = jax.ShapeDtypeStruct((CHUNK, width), BF16)
    low_rows = pltpu.VMEM((CHUNK, width), BF16)
    wide_rows = pltpu.VMEM((CHUNK, width), F32)
    tiles = pltpu.VMEM((span, CHUNK, block), BF16)
    return pl.pallas_call(
        body,
        grid_spec=pltpu.PrefetchScalarGridSpec(
            num_scalar_prefetch=3,
            grid=(1,),
            in_specs=[whole((4, width))] + any_specs(len(operands) - 1),
            out_specs=any_specs(3) + [whole((16, width))] + any_specs(3),
            scratch_shapes=[wide_rows, low_rows, low_rows, low_rows]
            + [pltpu.VMEM((CHUNK, HCAP), BF16)] * 2
            + [low_rows, wide_rows, low_rows, tiles, tiles, low_rows, wide_rows]
            + [
                panel.held(span * 3),
                pltpu.SemaphoreType.DMA((10 + span * (3 * panel.count + 2),)),
            ],
        ),
        out_shape=[
            jax.ShapeDtypeStruct(out_grad.shape, BF16),
            jax.ShapeDtypeStruct((CHUNK, width), F32),
            jax.ShapeDtypeStruct(out_grad.shape, BF16),
            jax.ShapeDtypeStruct((16, width), F32),
            wide_tile_shape,
            wide_tile_shape,
            low_shape,
        ],
        input_output_aliases={11 + i: out for i, out in enumerate((0, 2, 4, 5)[: len(before)])},
        compiler_params=params(),
        cost_estimate=cost(20),
        name="ffn_backward",
    )(panel.order, inner, group_weight, *operands)


def stack(refs):
    return jnp.concatenate([r[...] for r in refs], axis=0)


def turn(left, refs):
    left[...] = stack(refs).T


def grad_outputs(block, blocks, ranks, full=False):
    half = block // 2
    if full:
        return (
            pl.BlockSpec((2 * ranks, None, half // ranks, block), lambda s, *_: (0, s, 0, 0)),
            jax.ShapeDtypeStruct((2 * ranks, blocks, half // ranks, block), BF16),
        )
    if ranks is None:
        return (
            pl.BlockSpec((None, half, block), lambda s, *_: (s, 0, 0)),
            jax.ShapeDtypeStruct((blocks, half, block), BF16),
        )
    return (
        pl.BlockSpec((ranks, None, half // ranks, block), lambda s, *_: (0, s, 0, 0)),
        jax.ShapeDtypeStruct((ranks, blocks, half // ranks, block), BF16),
    )


def ffn_weight_grads(which, left, rights, ranks=None, arrived=None, full=False):
    length, width = left.shape
    block = width // 2
    half = block // 2
    span = HCAP // block
    per_row = len(rights) * span

    rows = block if full else half

    def body(core, g, *refs):
        out, turned = refs[-2:]
        step = pl.program_id(0) % per_row

        @pl.when(step == 0)
        def _():
            turned[...] = g[...].T

        def write(right):
            result = dot(turned[...], right[...])
            if arrived is not None:
                result = result + refs[len(rights)][...].astype(F32)
            out[...] = result.astype(BF16).reshape(out.shape)

        for i, right in enumerate(refs[: len(rights)]):
            pl.when(step // span == i)(lambda right=right: write(right))

    def right_spec(group):
        return pl.BlockSpec(
            (length, block), lambda s, core: (0, jnp.clip(s % per_row - group * span, 0, span - 1))
        )

    if full:
        left_spec = pl.BlockSpec((length, rows), lambda s, core: (0, s // per_row))
    else:
        left_spec = pl.BlockSpec((length, rows), lambda s, core: (0, s // per_row * 2 + core[0]))
    in_specs = [left_spec] + [right_spec(i) for i in range(len(rights))]
    operands = [left, *rights]
    blocks = width // block * per_row
    if arrived is not None:
        in_specs.append(pl.BlockSpec((None, half, block), lambda s, core: (s, 0, 0)))
        operands.append(arrived)
    out_spec, out_shape = grad_outputs(block, blocks, ranks, full)
    return pl.pallas_call(
        body,
        grid_spec=pltpu.PrefetchScalarGridSpec(
            num_scalar_prefetch=1,
            grid=(blocks,),
            in_specs=in_specs,
            out_specs=out_spec,
            scratch_shapes=[pltpu.VMEM((rows, length), BF16)],
        ),
        out_shape=out_shape,
        compiler_params=params(),
        cost_estimate=cost(15),
        name="ffn_weight_grads",
    )(which, *operands)


def halving_bits(ranks, row_block):
    bits = [1 << i for i in range(ranks.bit_length() - 1)]
    return bits if row_block % 2 == 0 else bits[::-1]


def halving_keys(ranks, row_block):
    bits = halving_bits(ranks, row_block)
    return [
        sum(bit for j, bit in enumerate(bits) if i >> (len(bits) - 1 - j) & 1) for i in range(ranks)
    ]


def attention_weight_grads(which, tokens, q_grad, k_grad, v_grad, attn_grad, context, ranks=None, arrived=None):
    length, width = tokens.shape
    chunks = len(context)
    local_width = k_grad.shape[1]
    block = 2 * local_width
    half = block // 2
    row_blocks = width // block
    outputs = 1 if ranks is None else 2 * row_blocks
    rows = half // (ranks or 1)

    def body(core, x, kg, vg, *refs):
        qg, ctx, g = (refs[i * chunks : (i + 1) * chunks] for i in range(3))
        refs = refs[3 * chunks :]
        outs, turned, held = refs[-2 - outputs : -2], refs[-2], refs[-1]
        row_block, step = pl.program_id(0) // 2, pl.program_id(0) % 2

        def write(start, right):
            cols = slice(start, start + local_width)
            result = dot(turned[...], right)
            if arrived is not None:
                result = result + refs[0][:, cols].astype(F32)
            result = result.astype(BF16)
            if ranks is None:
                outs[0][:, cols] = result
                return
            held[...] = result
            for r in range(row_blocks):

                @pl.when(row_block == r)
                def _(r=r):
                    for i, key in enumerate(halving_keys(ranks, r)):
                        own = span_of(core[1] ^ key, rows)
                        outs[2 * r + i // (ranks // 2)][i % (ranks // 2), :, cols] = held[own, :]

        @pl.when(step == 0)
        def _():
            turned[...] = x[...].T
            write(0, stack(qg))
            write(local_width, kg[...])

        @pl.when(step == 1)
        def _():
            write(0, vg[...])
            turn(turned, g)
            write(local_width, stack(ctx))

    in_specs = [pl.BlockSpec((length, half), lambda s, core: (0, s // 2 * 2 + core[0]))]
    in_specs += [whole((length, local_width))] * 2
    in_specs += [whole((CHUNK, local_width))] * (2 * chunks)
    in_specs += [pl.BlockSpec((CHUNK, half), lambda s, core: (0, s // 2 * 2 + core[0]))] * chunks
    operands = [tokens, k_grad, v_grad, *q_grad, *context, *attn_grad]
    if arrived is not None:
        in_specs.append(pl.BlockSpec((None, half, block), lambda s, core: (s, 0, 0)))
        operands.append(arrived)
    if ranks is None:
        out_specs = [pl.BlockSpec((None, half, block), lambda s, *_: (s, 0, 0))]
        out_shape = [jax.ShapeDtypeStruct((2 * row_blocks, half, block), BF16)]
    else:
        out_specs = [
            pl.BlockSpec(
                (ranks // 2, None, rows, block), lambda s, *_, r=i // 2: (0, jnp.clip(s - 2 * r, 0, 1), 0, 0)
            )
            for i in range(outputs)
        ]
        out_shape = [jax.ShapeDtypeStruct((ranks // 2, 2, rows, block), BF16)] * outputs
    return pl.pallas_call(
        body,
        grid_spec=pltpu.PrefetchScalarGridSpec(
            num_scalar_prefetch=1,
            grid=(2 * row_blocks,),
            in_specs=in_specs,
            out_specs=out_specs,
            scratch_shapes=[pltpu.VMEM((half, length), BF16), pltpu.VMEM((half, local_width), BF16)],
        ),
        out_shape=out_shape,
        compiler_params=params(),
        cost_estimate=cost(9),
        name="attention_weight_grads",
    )(which, *operands)


SWAP = [(0, 1), (1, 0)]


class Group:
    def __init__(self, grads):
        self.grads = grads
        self.core = lax.axis_index("obj").astype(jnp.int32).reshape(1)

    def make_away(self, *others):
        self.away = self.grads(after(1 - self.core, *others), None, None)
        return self.away

    def send(self, *others):
        self.arrived = lax.ppermute(after(self.away, *others), "obj", SWAP)
        return self.away

    def reduce(self, earlier, *others):
        own = self.grads(self.core, lax.axis_size("dp"), after(self.arrived, *others))
        operand = after(own, *[group.sum for group in earlier])
        self.sum = lax.psum_scatter(operand, "dp", scatter_dimension=0, tiled=True)[0]
        return own

    def reduce_whole(self, *others):
        own = self.grads(after(self.core, *others), lax.axis_size("dp"), None, True)
        self.sum = lax.psum_scatter(own, ("obj", "dp"), scatter_dimension=0, tiled=True)[0]
        return own


def pick_slices(places, groups, sizes):
    rows, block = groups[0].shape[1:]
    ends, total = [], 0
    for group in groups:
        total += group.shape[0]
        ends.append(total)
    targets = [(array, place) for array, size in enumerate(sizes) for place in range(size)]

    def body(place, *refs):
        sources, outs = refs[: len(groups)], refs[len(groups) : -3]
        held, into, out_of = refs[-3:]
        for i in range(len(targets)):
            for g, source in enumerate(sources):
                first = ends[g - 1] if g else 0

                @pl.when((place[i] >= first) & (place[i] < ends[g]))
                def _(source=source, first=first, i=i):
                    pltpu.make_async_copy(source.at[place[i] - first], held.at[i], into.at[i]).start()

        copies = []
        for i, (array, spot) in enumerate(targets):
            pltpu.make_async_copy(sources[0].at[0], held.at[i], into.at[i]).wait()
            copy = pltpu.make_async_copy(held.at[i], outs[array].at[spot], out_of.at[i])
            copy.start()
            copies.append(copy)
        wait_all(copies)

    return pl.pallas_call(
        body,
        grid_spec=pltpu.PrefetchScalarGridSpec(
            num_scalar_prefetch=1,
            grid=(1,),
            in_specs=any_specs(len(groups)),
            out_specs=any_specs(len(sizes)),
            scratch_shapes=[pltpu.VMEM((len(targets), rows, block), BF16)]
            + [pltpu.SemaphoreType.DMA((len(targets),))] * 2,
        ),
        out_shape=[jax.ShapeDtypeStruct((size, rows, block), BF16) for size in sizes],
        compiler_params=params(),
        cost_estimate=cost(5),
        name="pick_slices",
    )(places, *groups)


def place_blocks(starts, sources):
    slices, count, rows, block = sources[0].shape
    total = len(sources) * slices

    def body(begin, *refs):
        parts, out, held, into, out_of = refs[:-4], *refs[-4:]
        arriving, leaving = [], []
        for i in range(total):
            copy = pltpu.make_async_copy(parts[i // slices].at[i % slices], held.at[i], into.at[i])
            copy.start()
            arriving.append(copy)
        for i in range(total):
            arriving[i].wait()
            own = pl.ds(pl.multiple_of(begin[i], rows), rows)
            for j in range(count):
                target = out.at[i // slices // 2 * count + j, own]
                copy = pltpu.make_async_copy(held.at[i, j], target, out_of.at[i * count + j])
                copy.start()
                leaving.append(copy)
        wait_all(leaving)

    return pl.pallas_call(
        body,
        grid_spec=pltpu.PrefetchScalarGridSpec(
            num_scalar_prefetch=1,
            grid=(1,),
            in_specs=any_specs(len(sources)),
            out_specs=pl.BlockSpec(memory_space=pl.ANY),
            scratch_shapes=[
                pltpu.VMEM((total, count, rows, block), BF16),
                pltpu.SemaphoreType.DMA((total,)),
                pltpu.SemaphoreType.DMA((total * count,)),
            ],
        ),
        out_shape=jax.ShapeDtypeStruct((len(sources) // 2 * count, block, block), BF16),
        compiler_params=params(),
        cost_estimate=cost(6),
        name="place_blocks",
    )(starts, *sources)


def gather_block(starts, slices, grad):
    for i, piece in enumerate(slices):
        rows = piece.shape[0]
        grad[pl.ds(pl.multiple_of(starts[i], rows), rows), :] = piece[...]


def update_blocks(first, starts, scales, slices, roots_left, roots_right, weights, stats_left, stats_right, before):
    count, piece_rows, block = slices[0].shape
    half = block // 2
    steps = 4

    def body(begin, factor, *refs):
        pieces, refs = refs[: len(slices)], refs[len(slices) :]
        left, right, w, sl, sr = refs[:5]
        c_out, w_out, l_out, r_out, grad, inner, shaped, trust = refs[5 + len(before) :]
        slot, part = pl.program_id(0) + first, pl.program_id(1)
        clip = factor[0, slot]

        @pl.when(part == 0)
        def _():
            gather_block(begin, pieces, grad)
            low = (grad[...].astype(F32) * clip).astype(BF16)
            inner[...] = dot(left[...], low).astype(BF16)

        @pl.when(part == 1)
        def _():
            value = dot(inner[...], right[...])
            shaped[...] = value
            energy = jnp.sum(value * value) * (1.0 / (block * block))
            trust[...] = factor[2, slot] / jnp.sqrt(jnp.full((8, 128), energy, F32) + 1e-06)

        @pl.when(part >= 2)
        def _():
            rows = pl.ds(pl.multiple_of((part - 2) * half, half), half)
            w_out[...] = w[...] - trust[0:1, 0:1] * shaped[rows, :]
            own = grad[rows, :]
            c_out[...] = own.astype(F32) * clip
            square = factor[1, slot]
            l_out[...] = stat_decay * sl[...] + square * dot_nt(own, grad[...])
            r_out[...] = stat_decay * sr[...] + square * dot_tn(grad[:, rows], grad[...])

    def ahead(from_step):
        return lambda s, p, *_: jnp.minimum(s + (p >= from_step).astype(jnp.int32), count - 1)

    def full(place):
        return pl.BlockSpec((None, block, block), lambda s, p, *_: (first + place(s, p), 0, 0))

    piece = pl.BlockSpec((None, piece_rows, block), lambda s, p, *_: (ahead(3)(s, p), 0, 0))
    right_place = lambda s, p: jnp.maximum(s - (p < 1).astype(jnp.int32), 0)
    half_spec = pl.BlockSpec((None, half, block), lambda s, p, *_: (first + s, jnp.maximum(p - 2, 0), 0))
    out = jax.ShapeDtypeStruct(weights.shape, F32)
    in_specs = [piece] * len(slices) + [full(ahead(3)), full(right_place)] + [half_spec] * 3
    return pl.pallas_call(
        body,
        grid_spec=pltpu.PrefetchScalarGridSpec(
            num_scalar_prefetch=2,
            grid=(count, steps),
            in_specs=in_specs + any_specs(len(before)),
            out_specs=[half_spec] * 4,
            scratch_shapes=[
                pltpu.VMEM((block, block), BF16),
                pltpu.VMEM((block, block), BF16),
                pltpu.VMEM((block, block), F32),
                pltpu.VMEM((8, 128), F32),
            ],
        ),
        out_shape=[out] * 4,
        input_output_aliases={2 + len(in_specs) + i: i for i in range(len(before))},
        compiler_params=params(),
        cost_estimate=cost(14 * count),
        name="update_blocks",
    )(starts, scales, *slices, roots_left, roots_right, weights, stats_left, stats_right, *before)


def norm_sums(sums):
    return jnp.sum(sum(sums).reshape(2, 8, -1), axis=1)


def per_device(
    layer_input,
    out_grad,
    segment_ids,
    target_flags,
    hidden_units,
    block_slot,
    weight_blocks,
    stats_left,
    stats_right,
    roots_left,
    roots_right,
    norm_params,
    norm_moments,
):
    row_count, length, width = layer_input.shape
    local_width = HEADS // lax.axis_size("mp") * HD
    owned_slots, block = weight_blocks.shape[1], weight_blocks.shape[-1]
    half = block // 2
    slots = block_slot.shape[1]
    core = lax.axis_index("obj")

    master = weight_blocks[0]
    ranks, rank = lax.axis_size("dp"), lax.axis_index("dp").astype(jnp.int32)
    rows, row_blocks = half // ranks, width // block
    core_row = core.astype(jnp.int32) * half
    received_slices = [None] * ranks
    for k in [*range(1, ranks), 0]:
        first_row = core_row + (rank ^ k) * rows
        piece = lax.dynamic_slice(master, (0, first_row, 0), (owned_slots, rows, block)).astype(BF16)
        received_slices[k] = lax.ppermute(piece, "dp", [(i, i ^ k) for i in range(ranks)]) if k else piece
    by_place = block_slot[0].reshape(row_blocks, -1)
    attention_blocks = 4 * local_width // block
    panel_slots = jnp.concatenate([by_place[:, :attention_blocks].reshape(-1), by_place[:, attention_blocks:].reshape(-1)])
    weight_energy = jnp.mean(master * master, axis=(1, 2))
    low_left, low_right = roots_left[0].astype(BF16), roots_right[0].astype(BF16)
    sources = ((panel_slots // owned_slots) ^ rank) * owned_slots + panel_slots % owned_slots
    sources, weight_energy, low_left, low_right = lax.optimization_barrier(
        (sources, weight_energy, low_left, low_right)
    )
    sizes = [attention_blocks] * row_blocks + [slots - attention_blocks * row_blocks]
    *attention_slices, hidden_slices = pick_slices(sources, received_slices, sizes)
    hidden_panel = HiddenPanel(
        lax.all_gather(hidden_slices, ("obj", "dp"), axis=0), block_slot[0], row_blocks
    )
    parts_held, part_starts = [], []
    for row_block, held in enumerate(attention_slices):
        held, keys = held[None], [0]
        bits = [1 << i for i in range(ranks.bit_length() - 1)]
        for bit in bits if row_block % 2 == 0 else bits[::-1]:
            arriving = lax.ppermute(held, "dp", [(i, i ^ bit) for i in range(ranks)])
            held = jnp.concatenate([held, arriving])
            keys = keys + [key ^ bit for key in keys]
        parts_held += [held, lax.ppermute(held, "obj", SWAP)]
        first_rows = (rank ^ jnp.array(keys, jnp.int32)) * rows
        part_starts += [core_row + first_rows, half - core_row + first_rows]
    panel = Panel(place_blocks(jnp.concatenate(part_starts), parts_held), block_slot[0], row_blocks)

    flags = target_flags.reshape(length)
    own_count = jnp.sum(flags.astype(F32))
    total_count = axis_sum(own_count, ("obj", "dp"))
    group_total = lax.axis_size("obj") * lax.axis_size("dp")
    group_weight = own_count * group_total / total_count

    segments = segment_ids.reshape(length)
    cosine, sine = rotary_tables(segment_positions(segment_ids)[0])
    cosine, group_weight = lax.optimization_barrier((cosine, group_weight))
    index = jnp.arange(length, dtype=jnp.int32)
    in_span = (flags == 1) & (core == 1)
    key_col = jnp.where(in_span, index, -1)[:, None]
    col_key = jnp.where(in_span, index, -1)[None, :]

    tokens = layer_input.reshape(length, width)
    chunks = range(length // CHUNK)
    parts = [slice(c * CHUNK, (c + 1) * CHUNK) for c in chunks]
    query, keys_rot, values = qkv_forward(panel, tokens, cosine, sine, local_width)
    masks = (segments[:, None], segments[None, :], key_col, col_key)
    attended = [attend(panel, c, query, keys_rot, values, *masks) for c in chunks]
    probs, context, attn_part = zip(*attended)
    place = lax.axis_index("mp")
    inner_flag = ((place == 1) | (place == 2)).astype(jnp.int32).reshape(1)
    scalars = jnp.concatenate([inner_flag, hidden_units])
    weight_scalar = group_weight.reshape(1)
    flat_out_grad = out_grad.reshape(length, width)
    attn, ahead, back, turned = {}, {}, {}, {}

    def ffn_ahead(c, total, sent):
        attn[c] = (total, sent)
        before = [ahead[c - 1][i] for i in (1, 4)] if c else []
        ahead[c] = ffn_forward(hidden_panel, c, scalars, tokens, norm_params, total, sent, before)
        return ahead[c][5]

    def ffn_back(c, total, sent):
        hidden, _, act, slope, _, _ = ahead[c]
        saved = (hidden, norm_params, total, sent, flat_out_grad, act, slope)
        before = [back[c - 1][i] for i in (0, 2, 4, 5)] if c else []
        back[c] = ffn_backward(hidden_panel, c, inner_flag, weight_scalar, *saved, before)
        return back[c][6]

    def attention_back(c, total, sent):
        if c == len(chunks) - 1:
            total = after(total, down.sum)
        state = (tokens, norm_params, attn[c], back[c][1], (total, sent))
        heads = (query, keys_rot, values, probs[c], context[c], cosine, sine)
        carried = turned[c - 1][4] if c else None
        g1_before = turned[c - 1][0] if c else None
        last = c == len(chunks) - 1
        turned[c] = attend_backward(panel, c, last, inner_flag, state, *heads, carried, g1_before)
        return turned[c][2]

    def each_of(results, i):
        return [results[c][i] for c in chunks]

    last_chunk = chunks[-1]

    def down_grads(which, *opts):
        return ffn_weight_grads(which, back[last_chunk][2], [ahead[last_chunk][4]], *opts)

    def gate_up_grads(which, *opts):
        return ffn_weight_grads(which, ahead[last_chunk][1], list(back[last_chunk][4:6]), *opts)

    def attention_grads(which, *opts):
        heads = (each_of(turned, 3), *turned[chunks[-1]][4], each_of(turned, 1), context)
        return attention_weight_grads(which, tokens, *heads, *opts)

    down, gate_up = Group(down_grads), Group(gate_up_grads)

    first = len(chunks) - 1 + 2 * CYCLE
    before = {
        first: down.reduce_whole,
        first + 1: gate_up.send,
        first + 2: lambda *others: gate_up.reduce((), *others),
    }
    behind = {first: gate_up.make_away}
    run_slots(attn_part, (ffn_ahead, ffn_back, attention_back), inner_flag[0] == 1, before, behind)
    y_out = back[chunks[-1]][0].reshape(row_count, length, width)
    sums_two = each_of(back, 3)
    sums_one, query_grad = each_of(turned, 2), each_of(turned, 3)
    def squares(value):
        wide = value.astype(F32)
        return jnp.sum(wide * wide)

    own_core = core.astype(jnp.int32)
    (away,) = attention_grads(jnp.stack([1 - own_core, rank]))
    arrived = lax.ppermute(away, "obj", SWAP)
    input_part = input_parts(panel, [after(query_grad[0], away)] + query_grad[1:], *turned[chunks[-1]][4])
    own_norm_grad = jnp.concatenate([norm_sums(sums_one), norm_sums(sums_two)])
    norm_grad = axis_sum(after(own_norm_grad, away), ("obj", "dp"))
    halved = attention_grads(jnp.stack([own_core, rank]), ranks, after(arrived, input_part, norm_grad))
    early_squares = squares(gate_up.sum) + squares(down.sum)
    attention_sums = []
    for row_block in range(row_blocks):
        kept, sent = halved[2 * row_block : 2 * row_block + 2]
        for bit in halving_bits(ranks, row_block):
            arriving = lax.ppermute(sent, "dp", [(i, i ^ bit) for i in range(ranks)])
            if kept.shape[0] == 1:
                arriving = after(arriving, early_squares)
            total = kept + arriving
            kept, sent = total[: total.shape[0] // 2], total[total.shape[0] // 2 :]
        attention_sums.append(total[0])
    input_sum = lax.psum(after(input_part, gate_up.sum), "mp")

    groups = (*attention_sums, gate_up.sum, down.sum)
    own_squares = axis_sum(early_squares + sum(squares(group) for group in attention_sums), ("mp",))
    others = rank ^ jnp.arange(ranks, dtype=jnp.int32)
    col_blocks = slots // (width // block)
    place_of, firsts, base = [0] * slots, (0, 2, 2 + 2 * (HCAP // block), col_blocks), 0
    for first, stop in zip(firsts, firsts[1:]):
        for row_block in range(width // block):
            for col_block in range(first, stop):
                place_of[row_block * col_blocks + col_block] = base
                base += 1
    slot_index = jnp.arange(slots, dtype=jnp.int32)
    at_slot = jnp.sum(
        jnp.where(block_slot[0][None, :] == slot_index[:, None], jnp.array(place_of, jnp.int32)[None, :], 0),
        axis=1,
    )
    wanted = jnp.take(at_slot.reshape(ranks, owned_slots), others, axis=0).reshape(-1)
    halves = 2 if owned_slots % 2 == 0 else 1
    each = owned_slots // halves
    wanted = wanted.reshape(ranks, halves, each).transpose(1, 0, 2).reshape(-1)
    picked = pick_slices(wanted, groups, [each] * (halves * ranks))
    first_rows = others * rows
    starts = jnp.concatenate([core_row + first_rows, half - core_row + first_rows])
    low_roots = (low_left, low_right)

    def exchange(part, *earlier):
        pieces = [after(piece, *earlier) for piece in picked[part * ranks : (part + 1) * ranks]]
        mine = [
            lax.ppermute(piece, "dp", [(i, i ^ k) for i in range(ranks)]) if k else piece
            for k, piece in enumerate(pieces)
        ]
        return mine

    def hand_over(mine):
        return mine + [lax.ppermute(piece, "obj", SWAP) for piece in mine]

    rank_squares = [own_squares] + [
        lax.ppermute(own_squares, "dp", [(i, i ^ k) for i in range(ranks)]) for k in range(1, ranks)
    ]
    core_squares = jnp.sum(jnp.stack(rank_squares)[others])
    block_squares = axis_sum(core_squares, ("obj",))
    grad_norm = jnp.sqrt(block_squares + jnp.sum(norm_grad * norm_grad))
    clip_factor = 1.0 / jnp.maximum(grad_norm, 1.0)

    exchanged = [exchange(0, *rank_squares)]
    if halves == 2:
        exchanged.append(exchange(1, *exchanged[0], clip_factor))
    clips = jnp.full((owned_slots,), clip_factor, F32)
    scales = jnp.stack([clips, (1.0 - stat_decay) * clips * clips, block_rate * jnp.sqrt(weight_energy)])
    results = ()
    for part in range(halves):
        slices = hand_over([after(piece, *results[:1]) for piece in exchanged[part]])
        results = update_blocks(
            part * each, starts, scales, slices, *low_roots, master, stats_left[0], stats_right[0], results
        )
    clipped, new_weights, new_left, new_right = results
    x_grad = (deep_alpha * turned[chunks[-1]][0] + input_sum.astype(F32)).astype(BF16)
    x_grad = x_grad.reshape(row_count, length, width)
    param_clipped = norm_grad * clip_factor
    new_moments = 0.5 * norm_moments + 0.5 * param_clipped * param_clipped
    new_params = norm_params - param_rate * param_clipped / (jnp.sqrt(new_moments) + 1e-08)
    return (
        y_out,
        x_grad,
        clipped[None],
        new_weights[None],
        new_left[None],
        new_right[None],
        param_clipped,
        new_moments,
        new_params,
        grad_norm,
    )


def solution(mesh):
    return jax.shard_map(
        per_device,
        mesh=mesh,
        in_specs=(
            P(("obj", "dp"), None, None),
            P(("obj", "dp"), None, None),
            P(("obj", "dp"), None),
            P(("obj", "dp"), None),
            P("mp"),
            P("mp", None),
            P("mp", "dp", None, None),
            P("mp", "dp", None, None),
            P("mp", "dp", None, None),
            P("mp", "dp", None, None),
            P("mp", "dp", None, None),
            P(),
            P(),
        ),
        out_specs=(
            P(("obj", "dp"), None, None),
            P(("obj", "dp"), None, None),
            P("mp", "dp", None, None),
            P("mp", "dp", None, None),
            P("mp", "dp", None, None),
            P("mp", "dp", None, None),
            P(),
            P(),
            P(),
            P(),
        ),
        check_vma=False,
    )
```

time: 2800 us -> 797 us (0.28)
  waiting for transfers between devices: 1580 us -> 154 us
  matrix products: 421 us -> 0 us
  local copies, waits for them, and re-layouts: 411 us -> 18.7 us
  Pallas kernels: 0 us -> 385 us
  other arithmetic: 267 us -> 94.4 us
  starting transfers between devices: 0.29 us -> 108 us
  blocking collectives: 82 us -> 0 us
    psum x5 -> x1, waiting for transfers between devices: 734 us -> 0.02 us  [per_device(): input_sum = lax.psum(after(input_part, gate_up.sum), 'mp')]
    reduce_scatter x1, waiting for transfers between devices: 557 us -> 0.01 us  [reduce_whole(): lax.psum_scatter(own, ('obj', 'dp'), scatter_dimension=0, tiled=True)[0]]
    dot_general x22 -> x0, matrix products: 421 us -> none  [the longest x1 62.8 us: per_device(): jnp.einsum('bij,bjk->bik', roots_left[0], clipped, precision=highest)]
    pallas_call x0 -> x28, Pallas kernels: none -> 385 us  [the longest x2 72.3 us: update_blocks(): pl.pallas_call(body, grid_spec=pltpu.PrefetchScalarGridSpec(num_scalar_pr...]
    all_gather x1, waiting for transfers between devices: 293 us -> 0.01 us  [per_device(): lax.all_gather(hidden_slices, ('obj', 'dp'), axis=0)]
    gather x8 -> x3, local copies, waits for them, and re-layouts: 203 us -> 1.29 us  [the longest x2 0.65 us: per_device(): jnp.take(at_slot.reshape(ranks, owned_slots), others, axis=0).reshape(-1)]
    ppermute x0 -> x67, waiting for transfers between devices: none -> 154 us  [the longest x4 54.9 us: per_device(): arriving = lax.ppermute(held, 'dp', [(i, i ^ bit) for i in range(ranks)])]
    unnamed x96 -> x159, local copies, waits for them, and re-layouts: 133 us -> 7.1 us
  transfers between devices with their start and end apart: 7 -> 71, of which waited for: 7 -> 25; matrix products, arithmetic and copies ran while one was open for 3% -> 12% of each run, Pallas kernels for 0% -> 47%
where the time goes in v1:
time: 797 us; the launch traced here: 788 us
  Pallas kernels  385 us (48%)
  waiting for transfers between devices  154 us (19%)
  starting transfers between devices  108 us (14%)
  other arithmetic  94.4 us (12%)
  between operations  26.7 us (3%)
  local copies, waits for them, and re-layouts  18.7 us (2%)
    pallas_call x2, Pallas kernels, update_blocks(): pl.pallas_call(body, grid_spec=pltpu.PrefetchScalarGridSpec(num_scalar_pr...  72.3 us
    pallas_call x4, Pallas kernels, ffn_backward(): pl.pallas_call(body, grid_spec=pltpu.PrefetchScalarGridSpec(num_scalar_pr...  71.7 us
    pallas_call x4, Pallas kernels, ffn_forward(): pl.pallas_call(body, grid_spec=pltpu.PrefetchScalarGridSpec(num_scalar_pr...  60.8 us
    ppermute x4, waiting for transfers between devices, per_device(): arriving = lax.ppermute(held, 'dp', [(i, i ^ bit) for i in range(ranks)])  54.9 us
    ppermute x14, starting transfers between devices, run_slots(): paired = None if sending is None else lax.ppermute(sending, 'mp', PAIRS)  51 us
    pallas_call x4, Pallas kernels, attend_backward(): pl.pallas_call(body, grid_spec=pltpu.PrefetchScalarGridSpec(num_scalar_pr...  50.3 us
    pallas_call x3, Pallas kernels, ffn_weight_grads(): pl.pallas_call(body, grid_spec=pltpu.PrefetchScalarGridSpec(num_scalar_pr...  42.9 us
    ppermute x4, waiting for transfers between devices, per_device(): arriving = lax.ppermute(sent, 'dp', [(i, i ^ bit) for i in range(ranks)])  34.5 us
  transfers between devices with their start and end apart: 71, of which 25 were waited for; matrix products, arithmetic and copies ran while one was open for 12% of the time, Pallas kernels for 47%

profile of v1, /device:TPU:0, one launch (start us, length us, event | category | flops | bytes accessed | tf_op | source)
XLA Modules:
  0.0 787.6 jit_solution(8689331307921020899)
XLA Ops:
  18.7 17.9 %convert_bitcast_fusion = (bf16[4,1024,1024]{2,1,0:T(8,128)(2,1)}, bf16[4,1024,1024]{2,1,0:T(8,128)(2,1)}) fusion(f32[1,4,1024,1024]{3,2,1,0:T(8,128)} %param.26, f32[1,4,1024,1024]{3,2,1,0:T(8,128)} %param.25), kind=kLoop, calls=%fused_computation.3 | loop fusion | flops 8388608 | bytes 50331648 | tf_op jit(solution)/shard_map/convert_element_type | solution.py:1142
  45.4 16.4 %collective-permute-done.4.refs_2_ = bf16[4,128,1024]{2,1,0:T(8,128)(2,1)} collective-permute-done((bf16[4,128,1024]{2,1,0:T(8,128)(2,1)S(1)}, bf16[4,128,1024]{2,1,0:T(8,128)(2,1)}, u32[]{:S(2)}, u32[]{:S(2)}) %collective-permute-start.4) | collective-permute-done | bytes 1048608 | tf_op jit(solution)/shard_map/ppermute | solution.py:1137
  70.5 12.5 %collective-permute-done.6 = bf16[1,2,128,1024]{3,2,1,0:T(8,128)(2,1)S(1)} collective-permute-done((bf16[1,2,128,1024]{3,2,1,0:T(8,128)(2,1)S(1)}, bf16[1,2,128,1024]{3,2,1,0:T(8,128)(2,1)S(1)}, u32[]{:S(2)}, u32[]{:S(2)}) %collective-permute-start.6) | collective-permute-done | bytes 524320 | tf_op jit(solution)/shard_map/ppermute | solution.py:1157
  91.9 38.4 %collective-permute-done.7 = bf16[2,2,128,1024]{3,2,1,0:T(8,128)(2,1)} collective-permute-done((bf16[2,2,128,1024]{3,2,1,0:T(8,128)(2,1)S(1)}, bf16[2,2,128,1024]{3,2,1,0:T(8,128)(2,1)}, u32[]{:S(2)}, u32[]{:S(2)}) %collective-permute-start.7) | collective-permute-done | bytes 1048608 | tf_op jit(solution)/shard_map/ppermute | solution.py:1157
  160.1 11.6 %qkv_forward.1 = (bf16[768,512]{1,0:T(8,128)(2,1)}, bf16[768,512]{1,0:T(8,128)(2,1)}, bf16[768,512]{1,0:T(8,128)(2,1)}) custom-call(s32[16]{0:T(128)} %bitcast.159, bf16[768,2048]{1,0:T(8,128)(2,1)} %bitcast.125, f32[768,256]{1,0:T(8,128)} %pad_maximum_fusion.4.cos, f32[768,256]{1,0:T(8,128)} %pad_maximum_fusion.5.sin, bf16[8,512,1024]{2,1,0:T(8,128)(2,1)} %bitcast.80, ...), custom_call_target="tpu_custom_call" | custom-call | bytes 38500000 | tf_op jit(solution)/shard_map/qkv_forward/pallas_call | solution.py:256
  224.9 14.4 %collective-permute-start.16 = (bf16[192,2048]{1,0:T(8,128)(2,1)S(1)}, bf16[192,2048]{1,0:T(8,128)(2,1)S(1)}, u32[]{:S(2)}, u32[]{:S(2)}) collective-permute-start(bf16[192,2048]{1,0:T(8,128)(2,1)S(1)} %add_select_fusion.8.t_in.t1), channel_id=1, source_target_pairs={{0,1},{1,0},{2,3},{3,2},{4,5},{5,4},{6,7},{7,6},{8,9},{9,8},{10,11... | collective-permute-start | bytes 2359304 | tf_op jit(solution)/shard_map/ppermute | solution.py:147
  243.2 15.2 %ffn_forward.4 = (f32[192,2048]{1,0:T(8,128)}, bf16[768,2048]{1,0:T(8,128)(2,1)}, bf16[192,2048]{1,0:T(8,128)(2,1)}, bf16[192,2048]{1,0:T(8,128)(2,1)}, bf16[768...) custom-call(s32[16]{0:T(128)} %bitcast.164, s32[2]{0:T(128)} %pad_add_fusion.flags, f32[4,2048]{1,0:T(4,128)} %gains.23, ...), custom_call_target="tpu_custom_call" | custom-call | bytes 49000000 | tf_op jit(solution)/shard_map/ffn_forward/pallas_call | solution.py:608
  267.9 15.2 %ffn_forward.5 = (f32[192,2048]{1,0:T(8,128)}, bf16[768,2048]{1,0:T(8,128)(2,1)}, bf16[192,2048]{1,0:T(8,128)(2,1)}, bf16[192,2048]{1,0:T(8,128)(2,1)}, bf16[768...) custom-call(s32[16]{0:T(128)} %bitcast.165, s32[2]{0:T(128)} %pad_add_fusion.flags, ...), custom_call_target="tpu_custom_call", output_to_operand_aliasing={{1}: (7, {}), {4}: (8, {})} | custom-call | bytes 49000000 | tf_op jit(solution)/shard_map/ffn_forward/pallas_call | solution.py:608
  287.7 15.3 %ffn_forward.6 = (f32[192,2048]{1,0:T(8,128)}, bf16[768,2048]{1,0:T(8,128)(2,1)}, bf16[192,2048]{1,0:T(8,128)(2,1)}, bf16[192,2048]{1,0:T(8,128)(2,1)}, bf16[768...) custom-call(s32[16]{0:T(128)} %bitcast.166, s32[2]{0:T(128)} %pad_add_fusion.flags, ...), custom_call_target="tpu_custom_call", output_to_operand_aliasing={{1}: (7, {}), {4}: (8, {})} | custom-call | bytes 49000000 | tf_op jit(solution)/shard_map/ffn_forward/pallas_call | solution.py:608
  311.9 15.2 %ffn_forward.7 = (f32[192,2048]{1,0:T(8,128)}, bf16[768,2048]{1,0:T(8,128)(2,1)}, bf16[192,2048]{1,0:T(8,128)(2,1)}, bf16[192,2048]{1,0:T(8,128)(2,1)}, bf16[768...) custom-call(s32[16]{0:T(128)} %bitcast.167, s32[2]{0:T(128)} %pad_add_fusion.flags, ...), custom_call_target="tpu_custom_call", output_to_operand_aliasing={{1}: (7, {}), {4}: (8, {})} | custom-call | bytes 49000000 | tf_op jit(solution)/shard_map/ffn_forward/pallas_call | solution.py:608
  331.3 18.0 %ffn_backward.4 = (bf16[768,2048]{1,0:T(8,128)(2,1)}, f32[192,2048]{1,0:T(8,128)}, bf16[768,2048]{1,0:T(8,128)(2,1)}, f32[16,2048]{1,0:T(8,128)}, bf16[768,2048]...) custom-call(s32[16]{0:T(128)} %bitcast.168, s32[1]{0:T(128)} %bitcast.1.flags.flag, ...), custom_call_target="tpu_custom_call" | custom-call | bytes 70000000 | tf_op jit(solution)/shard_map/ffn_backward/pallas_call | solution.py:708
  357.2 17.9 %ffn_backward.5 = (bf16[768,2048]{1,0:T(8,128)(2,1)}, f32[192,2048]{1,0:T(8,128)}, bf16[768,2048]{1,0:T(8,128)(2,1)}, f32[16,2048]{1,0:T(8,128)}, bf16[768,2048]...) custom-call(s32[16]{0:T(128)} %bitcast.169, ...), custom_call_target="tpu_custom_call", output_to_operand_aliasing={{0}: (11, {}), {2}: (12, {}), {4}: (13, {}), {5}: (14, {})} | custom-call | bytes 70000000 | tf_op jit(solution)/shard_map/ffn_backward/pallas_call | solution.py:708
  379.5 18.0 %ffn_backward.6 = (bf16[768,2048]{1,0:T(8,128)(2,1)}, f32[192,2048]{1,0:T(8,128)}, bf16[768,2048]{1,0:T(8,128)(2,1)}, f32[16,2048]{1,0:T(8,128)}, bf16[768,2048]...) custom-call(s32[16]{0:T(128)} %bitcast.170, ...), custom_call_target="tpu_custom_call", output_to_operand_aliasing={{0}: (11, {}), {2}: (12, {}), {4}: (13, {}), {5}: (14, {})} | custom-call | bytes 70000000 | tf_op jit(solution)/shard_map/ffn_backward/pallas_call | solution.py:708
  405.4 17.9 %ffn_backward.7 = (bf16[768,2048]{1,0:T(8,128)(2,1)}, f32[192,2048]{1,0:T(8,128)}, bf16[768,2048]{1,0:T(8,128)(2,1)}, f32[16,2048]{1,0:T(8,128)}, bf16[768,2048]...) custom-call(s32[16]{0:T(128)} %bitcast.171, ...), custom_call_target="tpu_custom_call", output_to_operand_aliasing={{0}: (11, {}), {2}: (12, {}), {4}: (13, {}), {5}: (14, {})} | custom-call | bytes 70000000 | tf_op jit(solution)/shard_map/ffn_backward/pallas_call | solution.py:708
  425.9 12.3 %ffn_weight_grads.3 = bf16[8,4,128,1024]{3,2,1,0:T(8,128)(2,1)} custom-call(s32[1]{0:T(128)} %bitcast.21.core, bf16[768,2048]{1,0:T(8,128)(2,1)} %get-tuple-element.278.g, bf16[768,2048]{1,0:T(8,128)(2,1)} %get-tuple-element.279.refs_0_), custom_call_target="tpu_custom_call" | custom-call | bytes 52500000 | tf_op jit(solution)/shard_map/ffn_weight_grads/pallas_call | solution.py:807
  440.8 13.0 %attend_backward.4 = (f32[768,2048]{1,0:T(8,128)}, bf16[192,2048]{1,0:T(8,128)(2,1)}, f32[16,2048]{1,0:T(8,128)}, bf16[192,512]{1,0:T(8,128)(2,1)}, f32[768,512]{1,0:T(8,128)}, /*index=5*/f32[768,512]{1,0:T(8,128)}) custom-call(s32[16]{0:T(128)} %bitcast.172, s32[1]{0:T(128)} %bitcast.1.flags.flag, bf16[768,2048]{1,0:T(8,128)(2,1)} %bitcast.130, ...), custom_call_target="tpu_custom_call" | custom-call | bytes 42000000 | tf_op jit(solution)/shard_map/attend_backward/pallas_call | solution.py:423
  453.8 14.5 %ffn_weight_grads.4 = bf16[8,512,1024]{2,1,0:T(8,128)(2,1)} custom-call(s32[1]{0:T(128)S(6)} %sub.35.core, bf16[768,2048]{1,0:T(8,128)(2,1)} %get-tuple-element.285.g, bf16[768,2048]{1,0:T(8,128)(2,1)} %get-tuple-element.286.refs_0_, bf16[768,2048]{1,0:T(8,128)(2,1)} %get-tuple-element.287.refs_1_), custom_call_target="tpu_custom_call" | custom-call | bytes 52500000 | tf_op jit(solution)/shard_map/ffn_weight_grads/pallas_call | solution.py:807
  477.3 12.1 %attend_backward.5 = (f32[768,2048]{1,0:T(8,128)}, bf16[192,2048]{1,0:T(8,128)(2,1)}, f32[16,2048]{1,0:T(8,128)}, bf16[192,512]{1,0:T(8,128)(2,1)}, f32[768,512]{1,0:T(8,128)}, /*index=5*/f32[768,512]{1,0:T(8,128)}) custom-call(s32[16]{0:T(128)} %bitcast.173, s32[1]{0:T(128)} %bitcast.1.flags.flag, ...), custom_call_target="tpu_custom_call", output_to_operand_aliasing={{0}: (22, {})} | custom-call | bytes 42000000 | tf_op jit(solution)/shard_map/attend_backward/pallas_call | solution.py:423
  495.6 16.2 %ffn_weight_grads.5 = bf16[4,8,128,1024]{3,2,1,0:T(8,128)(2,1)} custom-call(s32[1]{0:T(128)} %bitcast.21.core, bf16[768,2048]{1,0:T(8,128)(2,1)} %get-tuple-element.285.g, bf16[768,2048]{1,0:T(8,128)(2,1)} %get-tuple-element.286.refs_0_, bf16[768,2048]{1,0:T(8,128)(2,1)} %get-tuple-element.287.refs_1_, bf16[8,512,1024]{2,1,0:T(8,128)(2,1)} %collective-permute-done.38.refs_2_), custom_call_target="tpu_custom_call" | custom-call | bytes 52500000 | tf_op jit(solution)/shard_map/ffn_weight_grads/pallas_call | solution.py:807
  516.8 12.5 %attend_backward.6 = (f32[768,2048]{1,0:T(8,128)}, bf16[192,2048]{1,0:T(8,128)(2,1)}, f32[16,2048]{1,0:T(8,128)}, bf16[192,512]{1,0:T(8,128)(2,1)}, f32[768,512]{1,0:T(8,128)}, /*index=5*/f32[768,512]{1,0:T(8,128)}) custom-call(s32[16]{0:T(128)} %bitcast.174, s32[1]{0:T(128)} %bitcast.1.flags.flag, ...), custom_call_target="tpu_custom_call", output_to_operand_aliasing={{0}: (22, {})} | custom-call | bytes 42000000 | tf_op jit(solution)/shard_map/attend_backward/pallas_call | solution.py:423
  534.6 12.7 %attend_backward.7 = (f32[768,2048]{1,0:T(8,128)}, bf16[192,2048]{1,0:T(8,128)(2,1)}, f32[16,2048]{1,0:T(8,128)}, bf16[192,512]{1,0:T(8,128)(2,1)}, bf16[768,512]{1,0:T(8,128)(2,1)}, /*index=5*/bf16[768,512]{1,0:T(8,128)(2,1)}) custom-call(s32[16]{0:T(128)} %bitcast.175, s32[1]{0:T(128)} %bitcast.1.flags.flag, ...), custom_call_target="tpu_custom_call", output_to_operand_aliasing={{0}: (22, {})} | custom-call | bytes 42000000 | tf_op jit(solution)/shard_map/attend_backward/pallas_call | solution.py:423
  593.6 26.8 %collective-permute-done.43 = bf16[2,2,128,1024]{3,2,1,0:T(8,128)(2,1)S(1)} collective-permute-done((bf16[2,2,128,1024]{3,2,1,0:T(8,128)(2,1)}, bf16[2,2,128,1024]{3,2,1,0:T(8,128)(2,1)S(1)}, u32[]{:S(2)}, u32[]{:S(2)}) %collective-permute-start.43) | collective-permute-done | bytes 1048608 | tf_op jit(solution)/shard_map/ppermute | solution.py:1261
  695.4 36.0 %update_blocks.2 = (f32[4,1024,1024]{2,1,0:T(8,128)}, f32[4,1024,1024]{2,1,0:T(8,128)}, f32[4,1024,1024]{2,1,0:T(8,128)}, f32[4,1024,1024]{2,1,0:T(8,128)}) custom-call(s32[8]{0:T(128)} %pad_add_fusion.4.begin, f32[3,4]{1,0:T(4,128)} %pad_maximum_fusion.7.factor, bf16[2,128,1024]{2,1,0:T(8,128)(2,1)} %get-tuple-element.348.refs_0_, ...), custom_call_target="tpu_custom_call" | custom-call | bytes 98000000 | tf_op jit(solution)/shard_map/update_blocks/pallas_call | solution.py:1081
  736.7 36.3 %update_blocks.3 = (f32[4,1024,1024]{2,1,0:T(8,128)}, f32[4,1024,1024]{2,1,0:T(8,128)}, f32[4,1024,1024]{2,1,0:T(8,128)}, f32[4,1024,1024]{2,1,0:T(8,128)}) custom-call(s32[8]{0:T(128)} %pad_add_fusion.4.begin, f32[3,4]{1,0:T(4,128)} %pad_maximum_fusion.7.factor, ...), custom_call_target="tpu_custom_call", output_to_operand_aliasing={{0}: (15, {}), {1}: (16, {}), {2}: (17, {}), {3}: (18, {})} | custom-call | bytes 98000000 | tf_op jit(solution)/shard_map/update_blocks/pallas_call | solution.py:1081
  (404 shorter events, 325.0 us)
Async XLA Ops:
  7.2 236.1 %all-gather.3.cloned.1.call-start = ((), (), s32[]{:S(2)}) async-start(), calls=%async_computation.4 | async-start | bytes 28311552 | tf_op jit(solution)/shard_map/all_gather | solution.py:1150
  12.7 32.7 %collective-permute-start.3 = (bf16[4,128,1024]{2,1,0:T(8,128)(2,1)}, bf16[4,128,1024]{2,1,0:T(8,128)(2,1)S(1)}, u32[]{:S(2)}, u32[]{:S(2)}) collective-permute-start(bf16[4,128,1024]{2,1,0:T(8,128)(2,1)} %get-tuple-element.386), channel_id=1, source_target_pairs={{0,4},{4,0},{8,12},{12,8},{1,5},{5,1},{9,13},{13,9},{2,6},{6,2},{1... | collective-permute-start | bytes 3145736 | tf_op jit(solution)/shard_map/ppermute | solution.py:1137
  15.7 46.1 %collective-permute-start.4 = (bf16[4,128,1024]{2,1,0:T(8,128)(2,1)S(1)}, bf16[4,128,1024]{2,1,0:T(8,128)(2,1)}, u32[]{:S(2)}, u32[]{:S(2)}) collective-permute-start(bf16[4,128,1024]{2,1,0:T(8,128)(2,1)S(1)} %get-tuple-element.388), channel_id=1, source_target_pairs={{0,8},{4,12},{8,0},{12,4},{1,9},{5,13},{9,1},{13,5},{2,10},{6,14},... | collective-permute-start | bytes 3145736 | tf_op jit(solution)/shard_map/ppermute | solution.py:1137
  17.2 45.7 %collective-permute-start.5 = (bf16[4,128,1024]{2,1,0:T(8,128)(2,1)S(1)}, bf16[4,128,1024]{2,1,0:T(8,128)(2,1)}, u32[]{:S(2)}, u32[]{:S(2)}) collective-permute-start(bf16[4,128,1024]{2,1,0:T(8,128)(2,1)S(1)} %get-tuple-element.385), channel_id=1, source_target_pairs={{0,12},{4,8},{8,4},{12,0},{1,13},{5,9},{9,5},{13,1},{2,14},{6,10},... | collective-permute-start | bytes 3145736 | tf_op jit(solution)/shard_map/ppermute | solution.py:1137
  67.5 466.2 %reduce-scatter.5.cloned.1.call-start = ((), (), s32[]{:S(2)}) async-start(), calls=%async_computation.2 | async-start | bytes 9437184 | tf_op jit(solution)/shard_map/reduce_scatter | solution.py:940
  83.1 47.2 %collective-permute-start.7 = (bf16[2,2,128,1024]{3,2,1,0:T(8,128)(2,1)S(1)}, bf16[2,2,128,1024]{3,2,1,0:T(8,128)(2,1)}, u32[]{:S(2)}, u32[]{:S(2)}) collective-permute-start(bf16[2,2,128,1024]{3,2,1,0:T(8,128)(2,1)S(1)} %pad_maximum_fusion.2), channel_id=1, source_target_pairs={{0,8},{4,12},{8,0},{12,4},{1,9},{5,13},{9,1},{13,5},{2,10},{6,14},... | collective-permute-start | bytes 3145736 | tf_op jit(solution)/shard_map/ppermute | solution.py:1157
  87.2 46.8 %collective-permute-start.10 = (bf16[2,2,128,1024]{3,2,1,0:T(8,128)(2,1)}, bf16[2,2,128,1024]{3,2,1,0:T(8,128)(2,1)}, u32[]{:S(2)}, u32[]{:S(2)}) collective-permute-start(bf16[2,2,128,1024]{3,2,1,0:T(8,128)(2,1)} %pad_maximum_fusion.3), channel_id=1, source_target_pairs={{0,4},{4,0},{8,12},{12,8},{1,5},{5,1},{9,13},{13,9},{2,6},{6,2},{1... | collective-permute-start | bytes 3145736 | tf_op jit(solution)/shard_map/ppermute | solution.py:1157
  88.1 54.7 %collective-permute-start = (f32[]{:T(128)}, f32[]{:T(128)}, u32[]{:S(2)}, u32[]{:S(2)}) collective-permute-start(f32[]{:T(128)} %convert_reduce_fusion), channel_id=1, source_target_pairs={{0,16},{16,0},{1,17},{17,1},{2,18},{18,2},{3,19},{19,3},{4,20},{20... | collective-permute-start | bytes 20 | tf_op jit(solution)/shard_map/ppermute | solution.py:100
  224.9 33.5 %collective-permute-start.16 = (bf16[192,2048]{1,0:T(8,128)(2,1)S(1)}, bf16[192,2048]{1,0:T(8,128)(2,1)S(1)}, u32[]{:S(2)}, u32[]{:S(2)}) collective-permute-start(bf16[192,2048]{1,0:T(8,128)(2,1)S(1)} %add_select_fusion.8.t_in.t1), channel_id=1, source_target_pairs={{0,1},{1,0},{2,3},{3,2},{4,5},{5,4},{6,7},{7,6},{8,9},{9,8},{10,11... | collective-permute-start | bytes 2359304 | tf_op jit(solution)/shard_map/ppermute | solution.py:147
  349.6 25.5 %collective-permute-start.26 = (bf16[192,2048]{1,0:T(8,128)(2,1)S(1)}, bf16[192,2048]{1,0:T(8,128)(2,1)}, u32[]{:S(2)}, u32[]{:S(2)}) collective-permute-start(bf16[192,2048]{1,0:T(8,128)(2,1)S(1)} %add.270), channel_id=1, source_target_pairs={{1,2},{2,1},{5,6},{6,5},{9,10},{10,9},{13,14},{14,13},{17,18},{18,... | collective-permute-start | bytes 2359304 | tf_op jit(solution)/shard_map/ppermute | solution.py:146
  352.6 24.9 %collective-permute-start.29 = (bf16[192,2048]{1,0:T(8,128)(2,1)S(1)}, bf16[192,2048]{1,0:T(8,128)(2,1)S(1)}, u32[]{:S(2)}, u32[]{:S(2)}) collective-permute-start(bf16[192,2048]{1,0:T(8,128)(2,1)S(1)} %add_select_fusion.3.t_in), channel_id=1, source_target_pairs={{0,1},{1,0},{2,3},{3,2},{4,5},{5,4},{6,7},{7,6},{8,9},{9,8},{10,11... | collective-permute-start | bytes 2359304 | tf_op jit(solution)/shard_map/ppermute | solution.py:147
  397.8 25.6 %collective-permute-start.31 = (bf16[192,2048]{1,0:T(8,128)(2,1)S(1)}, bf16[192,2048]{1,0:T(8,128)(2,1)S(1)}, u32[]{:S(2)}, u32[]{:S(2)}) collective-permute-start(bf16[192,2048]{1,0:T(8,128)(2,1)S(1)} %add.275), channel_id=1, source_target_pairs={{1,2},{2,1},{5,6},{6,5},{9,10},{10,9},{13,14},{14,13},{17,18},{18,... | collective-permute-start | bytes 2359304 | tf_op jit(solution)/shard_map/ppermute | solution.py:146
  400.0 25.6 %collective-permute-start.33 = (bf16[192,2048]{1,0:T(8,128)(2,1)S(1)}, bf16[192,2048]{1,0:T(8,128)(2,1)S(1)}, u32[]{:S(2)}, u32[]{:S(2)}) collective-permute-start(bf16[192,2048]{1,0:T(8,128)(2,1)S(1)} %add_select_fusion.1.t3), channel_id=1, source_target_pairs={{0,1},{1,0},{2,3},{3,2},{4,5},{5,4},{6,7},{7,6},{8,9},{9,8},{10,11... | collective-permute-start | bytes 2359304 | tf_op jit(solution)/shard_map/ppermute | solution.py:147
  438.1 189.0 %reduce-scatter.7.cloned.1.call-start = ((), (), s32[]{:S(2)}) async-start(), calls=%async_computation.5 | async-start | bytes 10485760
  439.3 29.0 %collective-permute-start.32 = (bf16[192,2048]{1,0:T(8,128)(2,1)S(1)}, bf16[192,2048]{1,0:T(8,128)(2,1)S(1)}, u32[]{:S(2)}, u32[]{:S(2)}) collective-permute-start(bf16[192,2048]{1,0:T(8,128)(2,1)S(1)} %copy-done.34), channel_id=1, source_target_pairs={{0,1},{1,0},{2,3},{3,2},{4,5},{5,4},{6,7},{7,6},{8,9},{9,8},{10,11... | collective-permute-start | bytes 2359304 | tf_op jit(solution)/shard_map/ppermute | solution.py:147
  439.3 29.3 %collective-permute-start.35 = (bf16[192,2048]{1,0:T(8,128)(2,1)S(1)}, bf16[192,2048]{1,0:T(8,128)(2,1)}, u32[]{:S(2)}, u32[]{:S(2)}) collective-permute-start(bf16[192,2048]{1,0:T(8,128)(2,1)S(1)} %add.277), channel_id=1, source_target_pairs={{1,2},{2,1},{5,6},{6,5},{9,10},{10,9},{13,14},{14,13},{17,18},{18,... | collective-permute-start | bytes 2359304 | tf_op jit(solution)/shard_map/ppermute | solution.py:146
  470.1 25.4 %collective-permute-start.38 = (bf16[8,512,1024]{2,1,0:T(8,128)(2,1)}, bf16[8,512,1024]{2,1,0:T(8,128)(2,1)}, u32[]{:S(2)}, u32[]{:S(2)}) collective-permute-start(bf16[8,512,1024]{2,1,0:T(8,128)(2,1)} %ffn_weight_grads.4), channel_id=1, source_target_pairs={{0,16},{16,0},{1,17},{17,1},{2,18},{18,2},{3,19},{19,3},{4,20},{20... | collective-permute-start | bytes 25165832 | tf_op jit(solution)/shard_map/ppermute | solution.py:929
  471.1 24.4 %collective-permute-start.36 = (bf16[192,2048]{1,0:T(8,128)(2,1)S(1)}, bf16[192,2048]{1,0:T(8,128)(2,1)}, u32[]{:S(2)}, u32[]{:S(2)}) collective-permute-start(bf16[192,2048]{1,0:T(8,128)(2,1)S(1)} %add.279.t3), channel_id=1, source_target_pairs={{0,1},{1,0},{2,3},{3,2},{4,5},{5,4},{6,7},{7,6},{8,9},{9,8},{10,11... | collective-permute-start | bytes 2359304 | tf_op jit(solution)/shard_map/ppermute | solution.py:147
  511.8 261.2 %all-reduce.3.cloned.1.call-start = ((), (), s32[]{:S(2)}) async-start(), calls=%async_computation.3 | async-start | bytes 6291456 | tf_op jit(solution)/shard_map/psum | solution.py:1267
  590.6 29.8 %collective-permute-start.43 = (bf16[2,2,128,1024]{3,2,1,0:T(8,128)(2,1)}, bf16[2,2,128,1024]{3,2,1,0:T(8,128)(2,1)S(1)}, u32[]{:S(2)}, u32[]{:S(2)}) collective-permute-start(bf16[2,2,128,1024]{3,2,1,0:T(8,128)(2,1)} %get-tuple-element.340), channel_id=1, source_target_pairs={{0,4},{4,0},{8,12},{12,8},{1,5},{5,1},{9,13},{13,9},{2,6},{6,2},{1... | collective-permute-start | bytes 3145736 | tf_op jit(solution)/shard_map/ppermute | solution.py:1261
  591.4 33.0 %collective-permute-start.45 = (bf16[2,2,128,1024]{3,2,1,0:T(8,128)(2,1)}, bf16[2,2,128,1024]{3,2,1,0:T(8,128)(2,1)S(1)}, u32[]{:S(2)}, u32[]{:S(2)}) collective-permute-start(bf16[2,2,128,1024]{3,2,1,0:T(8,128)(2,1)} %get-tuple-element.343), channel_id=1, source_target_pairs={{0,8},{4,12},{8,0},{12,4},{1,9},{5,13},{9,1},{13,5},{2,10},{6,14},... | collective-permute-start | bytes 3145736 | tf_op jit(solution)/shard_map/ppermute | solution.py:1261
  691.0 40.4 %collective-permute-start.60 = (bf16[2,128,1024]{2,1,0:T(8,128)(2,1)}, bf16[2,128,1024]{2,1,0:T(8,128)(2,1)S(1)}, u32[]{:S(2)}, u32[]{:S(2)}) collective-permute-start(bf16[2,128,1024]{2,1,0:T(8,128)(2,1)} %get-tuple-element.361), channel_id=1, source_target_pairs={{0,4},{4,0},{8,12},{12,8},{1,5},{5,1},{9,13},{13,9},{2,6},{6,2},{1... | collective-permute-start | bytes 1572872 | tf_op jit(solution)/shard_map/ppermute | solution.py:1296
  691.9 39.5 %collective-permute-start.61 = (bf16[2,128,1024]{2,1,0:T(8,128)(2,1)}, bf16[2,128,1024]{2,1,0:T(8,128)(2,1)}, u32[]{:S(2)}, u32[]{:S(2)}) collective-permute-start(bf16[2,128,1024]{2,1,0:T(8,128)(2,1)} %get-tuple-element.364), channel_id=1, source_target_pairs={{0,8},{4,12},{8,0},{12,4},{1,9},{5,13},{9,1},{13,5},{2,10},{6,14},... | collective-permute-start | bytes 1572872 | tf_op jit(solution)/shard_map/ppermute | solution.py:1296
  693.1 38.3 %collective-permute-start.62 = (bf16[2,128,1024]{2,1,0:T(8,128)(2,1)}, bf16[2,128,1024]{2,1,0:T(8,128)(2,1)}, u32[]{:S(2)}, u32[]{:S(2)}) collective-permute-start(bf16[2,128,1024]{2,1,0:T(8,128)(2,1)} %get-tuple-element.367), channel_id=1, source_target_pairs={{0,12},{4,8},{8,4},{12,0},{1,13},{5,9},{9,5},{13,1},{2,14},{6,10},... | collective-permute-start | bytes 1572872 | tf_op jit(solution)/shard_map/ppermute | solution.py:1296
  (126 other events, 1599.7 us)
Sparse Core Ops, SparseCore 0:
  67.6 148.5 all-gather.2
  438.3 70.1 reduce-scatter.4
  512.4 91.8 reduce-scatter.6
  627.3 121.0 all-reduce.2

commit v2 on v1

--- a/solution.py
+++ b/solution.py
@@ -496,6 +496,14 @@
     ]
 
 
+def copy_received(copies, inner, total, sent, target):
+    sem = copies.sems.at[copies.count]
+    copies.count += 1
+    pl.when(inner == 1)(lambda: pltpu.make_async_copy(total, target, sem).start())
+    pl.when(inner != 1)(lambda: pltpu.make_async_copy(sent, target, sem).start())
+    return pltpu.make_async_copy(total, target, sem)
+
+
 class Copies:
     def __init__(self, sems):
         self.sems = sems
@@ -549,9 +557,9 @@
     def body(order, flags, gains, x_in, t_in, s_in, slices, *refs):
         refs = refs[len(before) :]
         hid_out, low_out, act_out, slope_out, inner_out, f_out = refs[:6]
-        x, t1, s1, hid, low, act, slope, inner, f, acc, held, sems = refs[6:]
+        x, t1, hid, low, act, slope, inner, f, acc, held, sems = refs[6:]
         copies = Copies(sems)
-        rows_in = [copies.start(a, b) for a, b in ((t_in, t1), (s_in, s1), (x_in.at[own], x))]
+        rows_in = [copy_received(copies, flags[0], t_in, s_in, t1), copies.start(x_in.at[own], x)]
         weights = {
             (tile, group): [
                 panel.copy(copies, slices, k, group * span + tile, held.at[tile * 3 + group])
@@ -563,7 +571,7 @@
         wait_all(rows_in)
 
         def norm_strip(rows):
-            resid = deep_alpha * x[rows, :].astype(F32) + received(flags, t1, s1, rows)
+            resid = deep_alpha * x[rows, :].astype(F32) + t1[rows, :].astype(F32)
             normed, _ = normalize(resid)
             value = normed * gains[0:1, :] + gains[1:2, :]
             hid[rows, :] = value
@@ -612,7 +620,7 @@
             grid=(1,),
             in_specs=[whole((4, width))] + any_specs(4 + len(before)),
             out_specs=any_specs(6),
-            scratch_shapes=[low_rows] * 3
+            scratch_shapes=[low_rows] * 2
             + [wide_rows, low_rows]
             + [tiles] * 3
             + [low_rows, wide_rows]
@@ -647,10 +655,10 @@
     def body(order, flags, scale, gains, hid_in, t_in, s_in, og_in, act_in, slope_in, slices, *refs):
         refs = refs[len(before) :]
         y_out, g2_out, low_out, sums, gate_out, up_out, h_out = refs[:7]
-        hid, t2, s2, og, act_rows, slope_rows, y, g2, low, gate, up, h, acc, held, sems = refs[7:]
+        hid, t2, og, act_rows, slope_rows, y, g2, low, gate, up, h, acc, held, sems = refs[7:]
         copies = Copies(sems)
-        pairs = ((t_in, t2), (s_in, s2), (hid_in, hid), (og_in.at[own], og))
-        rows_in = [copies.start(a, b) for a, b in pairs]
+        rows_in = [copies.start(hid_in, hid), copies.start(og_in.at[own], og)]
+        rows_in.append(copy_received(copies, flags[0], t_in, s_in, t2))
         saved = [copies.start(act_in, act_rows), copies.start(slope_in, slope_rows)]
         weights = {
             (tile, group): [
@@ -664,7 +672,7 @@
         wait_all(rows_in)
 
         def norm_strip(rows):
-            resid = deep_alpha * hid[rows, :] + received(flags, t2, s2, rows)
+            resid = deep_alpha * hid[rows, :] + t2[rows, :].astype(F32)
             normed, inverse = normalize(resid)
             y[rows, :] = (normed * gains[2:3, :] + gains[3:4, :]).astype(BF16)
             grad = scale[0] * og[rows, :].astype(F32)
@@ -712,7 +720,7 @@
             grid=(1,),
             in_specs=[whole((4, width))] + any_specs(len(operands) - 1),
             out_specs=any_specs(3) + [whole((16, width))] + any_specs(3),
-            scratch_shapes=[wide_rows, low_rows, low_rows, low_rows]
+            scratch_shapes=[wide_rows, low_rows, low_rows]
             + [pltpu.VMEM((CHUNK, HCAP), BF16)] * 2
             + [low_rows, wide_rows, low_rows, tiles, tiles, low_rows, wide_rows]
             + [

time: 797 us -> 795 us (level)
  no operation moved by 1% of the time
where the time goes in v2:
time: 795 us; the launch traced here: 786 us
  Pallas kernels  383 us (48%)
  waiting for transfers between devices  155 us (19%)
  starting transfers between devices  108 us (14%)
  other arithmetic  94.5 us (12%)
  between operations  26.7 us (3%)
  local copies, waits for them, and re-layouts  18.7 us (2%)
    pallas_call x2, Pallas kernels, update_blocks(): pl.pallas_call(body, grid_spec=pltpu.PrefetchScalarGridSpec(num_scalar_pr...  72.3 us
    pallas_call x4, Pallas kernels, ffn_backward(): pl.pallas_call(body, grid_spec=pltpu.PrefetchScalarGridSpec(num_scalar_pr...  70.7 us
    pallas_call x4, Pallas kernels, ffn_forward(): pl.pallas_call(body, grid_spec=pltpu.PrefetchScalarGridSpec(num_scalar_pr...  60 us
    ppermute x4, waiting for transfers between devices, per_device(): arriving = lax.ppermute(held, 'dp', [(i, i ^ bit) for i in range(ranks)])  54.9 us
    ppermute x14, starting transfers between devices, run_slots(): paired = None if sending is None else lax.ppermute(sending, 'mp', PAIRS)  50.8 us
    pallas_call x4, Pallas kernels, attend_backward(): pl.pallas_call(body, grid_spec=pltpu.PrefetchScalarGridSpec(num_scalar_pr...  50 us
    pallas_call x3, Pallas kernels, ffn_weight_grads(): pl.pallas_call(body, grid_spec=pltpu.PrefetchScalarGridSpec(num_scalar_pr...  43 us
    ppermute x4, waiting for transfers between devices, per_device(): arriving = lax.ppermute(sent, 'dp', [(i, i ^ bit) for i in range(ranks)])  35 us
  transfers between devices with their start and end apart: 71, of which 25 were waited for; matrix products, arithmetic and copies ran while one was open for 12% of the time, Pallas kernels for 47%

profile of v2, /device:TPU:0, one launch (start us, length us, event | category | flops | bytes accessed | tf_op | source)
XLA Modules:
  0.0 785.8 jit_solution(16725525775846338211)
XLA Ops:
  18.7 17.9 %convert_bitcast_fusion = (bf16[4,1024,1024]{2,1,0:T(8,128)(2,1)}, bf16[4,1024,1024]{2,1,0:T(8,128)(2,1)}) fusion(f32[1,4,1024,1024]{3,2,1,0:T(8,128)} %param.26, f32[1,4,1024,1024]{3,2,1,0:T(8,128)} %param.25), kind=kLoop, calls=%fused_computation.3 | loop fusion | flops 8388608 | bytes 50331648 | tf_op jit(solution)/shard_map/convert_element_type | solution.py:1150
  45.4 16.4 %collective-permute-done.4.refs_2_ = bf16[4,128,1024]{2,1,0:T(8,128)(2,1)} collective-permute-done((bf16[4,128,1024]{2,1,0:T(8,128)(2,1)S(1)}, bf16[4,128,1024]{2,1,0:T(8,128)(2,1)}, u32[]{:S(2)}, u32[]{:S(2)}) %collective-permute-start.4) | collective-permute-done | bytes 1048608 | tf_op jit(solution)/shard_map/ppermute | solution.py:1145
  70.5 12.5 %collective-permute-done.6 = bf16[1,2,128,1024]{3,2,1,0:T(8,128)(2,1)S(1)} collective-permute-done((bf16[1,2,128,1024]{3,2,1,0:T(8,128)(2,1)S(1)}, bf16[1,2,128,1024]{3,2,1,0:T(8,128)(2,1)S(1)}, u32[]{:S(2)}, u32[]{:S(2)}) %collective-permute-start.6) | collective-permute-done | bytes 524320 | tf_op jit(solution)/shard_map/ppermute | solution.py:1165
  91.9 38.4 %collective-permute-done.7 = bf16[2,2,128,1024]{3,2,1,0:T(8,128)(2,1)} collective-permute-done((bf16[2,2,128,1024]{3,2,1,0:T(8,128)(2,1)S(1)}, bf16[2,2,128,1024]{3,2,1,0:T(8,128)(2,1)}, u32[]{:S(2)}, u32[]{:S(2)}) %collective-permute-start.7) | collective-permute-done | bytes 1048608 | tf_op jit(solution)/shard_map/ppermute | solution.py:1165
  160.1 11.6 %qkv_forward.1 = (bf16[768,512]{1,0:T(8,128)(2,1)}, bf16[768,512]{1,0:T(8,128)(2,1)}, bf16[768,512]{1,0:T(8,128)(2,1)}) custom-call(s32[16]{0:T(128)} %bitcast.159, bf16[768,2048]{1,0:T(8,128)(2,1)} %bitcast.125, f32[768,256]{1,0:T(8,128)} %pad_maximum_fusion.4.cos, f32[768,256]{1,0:T(8,128)} %pad_maximum_fusion.5.sin, bf16[8,512,1024]{2,1,0:T(8,128)(2,1)} %bitcast.80, ...), custom_call_target="tpu_custom_call" | custom-call | bytes 38500000 | tf_op jit(solution)/shard_map/qkv_forward/pallas_call | solution.py:256
  224.9 14.3 %collective-permute-start.16 = (bf16[192,2048]{1,0:T(8,128)(2,1)S(1)}, bf16[192,2048]{1,0:T(8,128)(2,1)S(1)}, u32[]{:S(2)}, u32[]{:S(2)}) collective-permute-start(bf16[192,2048]{1,0:T(8,128)(2,1)S(1)} %add_select_fusion.8.t_in.t1), channel_id=1, source_target_pairs={{0,1},{1,0},{2,3},{3,2},{4,5},{5,4},{6,7},{7,6},{8,9},{9,8},{10,11... | collective-permute-start | bytes 2359304 | tf_op jit(solution)/shard_map/ppermute | solution.py:147
  243.2 15.0 %ffn_forward.4 = (f32[192,2048]{1,0:T(8,128)}, bf16[768,2048]{1,0:T(8,128)(2,1)}, bf16[192,2048]{1,0:T(8,128)(2,1)}, bf16[192,2048]{1,0:T(8,128)(2,1)}, bf16[768...) custom-call(s32[16]{0:T(128)} %bitcast.164, s32[2]{0:T(128)} %pad_add_fusion.flags, f32[4,2048]{1,0:T(4,128)} %gains.23, ...), custom_call_target="tpu_custom_call" | custom-call | bytes 49000000 | tf_op jit(solution)/shard_map/ffn_forward/pallas_call | solution.py:616
  267.6 15.0 %ffn_forward.5 = (f32[192,2048]{1,0:T(8,128)}, bf16[768,2048]{1,0:T(8,128)(2,1)}, bf16[192,2048]{1,0:T(8,128)(2,1)}, bf16[192,2048]{1,0:T(8,128)(2,1)}, bf16[768...) custom-call(s32[16]{0:T(128)} %bitcast.165, s32[2]{0:T(128)} %pad_add_fusion.flags, ...), custom_call_target="tpu_custom_call", output_to_operand_aliasing={{1}: (7, {}), {4}: (8, {})} | custom-call | bytes 49000000 | tf_op jit(solution)/shard_map/ffn_forward/pallas_call | solution.py:616
  287.1 15.1 %ffn_forward.6 = (f32[192,2048]{1,0:T(8,128)}, bf16[768,2048]{1,0:T(8,128)(2,1)}, bf16[192,2048]{1,0:T(8,128)(2,1)}, bf16[192,2048]{1,0:T(8,128)(2,1)}, bf16[768...) custom-call(s32[16]{0:T(128)} %bitcast.166, s32[2]{0:T(128)} %pad_add_fusion.flags, ...), custom_call_target="tpu_custom_call", output_to_operand_aliasing={{1}: (7, {}), {4}: (8, {})} | custom-call | bytes 49000000 | tf_op jit(solution)/shard_map/ffn_forward/pallas_call | solution.py:616
  311.1 15.0 %ffn_forward.7 = (f32[192,2048]{1,0:T(8,128)}, bf16[768,2048]{1,0:T(8,128)(2,1)}, bf16[192,2048]{1,0:T(8,128)(2,1)}, bf16[192,2048]{1,0:T(8,128)(2,1)}, bf16[768...) custom-call(s32[16]{0:T(128)} %bitcast.167, s32[2]{0:T(128)} %pad_add_fusion.flags, ...), custom_call_target="tpu_custom_call", output_to_operand_aliasing={{1}: (7, {}), {4}: (8, {})} | custom-call | bytes 49000000 | tf_op jit(solution)/shard_map/ffn_forward/pallas_call | solution.py:616
  330.2 17.8 %ffn_backward.4 = (bf16[768,2048]{1,0:T(8,128)(2,1)}, f32[192,2048]{1,0:T(8,128)}, bf16[768,2048]{1,0:T(8,128)(2,1)}, f32[16,2048]{1,0:T(8,128)}, bf16[768,2048]...) custom-call(s32[16]{0:T(128)} %bitcast.168, s32[1]{0:T(128)} %bitcast.1.flags.flag, ...), custom_call_target="tpu_custom_call" | custom-call | bytes 70000000 | tf_op jit(solution)/shard_map/ffn_backward/pallas_call | solution.py:716
  356.0 17.6 %ffn_backward.5 = (bf16[768,2048]{1,0:T(8,128)(2,1)}, f32[192,2048]{1,0:T(8,128)}, bf16[768,2048]{1,0:T(8,128)(2,1)}, f32[16,2048]{1,0:T(8,128)}, bf16[768,2048]...) custom-call(s32[16]{0:T(128)} %bitcast.169, ...), custom_call_target="tpu_custom_call", output_to_operand_aliasing={{0}: (11, {}), {2}: (12, {}), {4}: (13, {}), {5}: (14, {})} | custom-call | bytes 70000000 | tf_op jit(solution)/shard_map/ffn_backward/pallas_call | solution.py:716
  378.0 17.7 %ffn_backward.6 = (bf16[768,2048]{1,0:T(8,128)(2,1)}, f32[192,2048]{1,0:T(8,128)}, bf16[768,2048]{1,0:T(8,128)(2,1)}, f32[16,2048]{1,0:T(8,128)}, bf16[768,2048]...) custom-call(s32[16]{0:T(128)} %bitcast.170, ...), custom_call_target="tpu_custom_call", output_to_operand_aliasing={{0}: (11, {}), {2}: (12, {}), {4}: (13, {}), {5}: (14, {})} | custom-call | bytes 70000000 | tf_op jit(solution)/shard_map/ffn_backward/pallas_call | solution.py:716
  403.7 17.6 %ffn_backward.7 = (bf16[768,2048]{1,0:T(8,128)(2,1)}, f32[192,2048]{1,0:T(8,128)}, bf16[768,2048]{1,0:T(8,128)(2,1)}, f32[16,2048]{1,0:T(8,128)}, bf16[768,2048]...) custom-call(s32[16]{0:T(128)} %bitcast.171, ...), custom_call_target="tpu_custom_call", output_to_operand_aliasing={{0}: (11, {}), {2}: (12, {}), {4}: (13, {}), {5}: (14, {})} | custom-call | bytes 70000000 | tf_op jit(solution)/shard_map/ffn_backward/pallas_call | solution.py:716
  423.9 12.3 %ffn_weight_grads.3 = bf16[8,4,128,1024]{3,2,1,0:T(8,128)(2,1)} custom-call(s32[1]{0:T(128)} %bitcast.21.core, bf16[768,2048]{1,0:T(8,128)(2,1)} %get-tuple-element.278.g, bf16[768,2048]{1,0:T(8,128)(2,1)} %get-tuple-element.279.refs_0_), custom_call_target="tpu_custom_call" | custom-call | bytes 52500000 | tf_op jit(solution)/shard_map/ffn_weight_grads/pallas_call | solution.py:815
  438.8 12.8 %attend_backward.4 = (f32[768,2048]{1,0:T(8,128)}, bf16[192,2048]{1,0:T(8,128)(2,1)}, f32[16,2048]{1,0:T(8,128)}, bf16[192,512]{1,0:T(8,128)(2,1)}, f32[768,512]{1,0:T(8,128)}, /*index=5*/f32[768,512]{1,0:T(8,128)}) custom-call(s32[16]{0:T(128)} %bitcast.172, s32[1]{0:T(128)} %bitcast.1.flags.flag, bf16[768,2048]{1,0:T(8,128)(2,1)} %bitcast.130, ...), custom_call_target="tpu_custom_call" | custom-call | bytes 42000000 | tf_op jit(solution)/shard_map/attend_backward/pallas_call | solution.py:423
  451.6 14.5 %ffn_weight_grads.4 = bf16[8,512,1024]{2,1,0:T(8,128)(2,1)} custom-call(s32[1]{0:T(128)S(6)} %sub.35.core, bf16[768,2048]{1,0:T(8,128)(2,1)} %get-tuple-element.285.g, bf16[768,2048]{1,0:T(8,128)(2,1)} %get-tuple-element.286.refs_0_, bf16[768,2048]{1,0:T(8,128)(2,1)} %get-tuple-element.287.refs_1_), custom_call_target="tpu_custom_call" | custom-call | bytes 52500000 | tf_op jit(solution)/shard_map/ffn_weight_grads/pallas_call | solution.py:815
  475.2 12.0 %attend_backward.5 = (f32[768,2048]{1,0:T(8,128)}, bf16[192,2048]{1,0:T(8,128)(2,1)}, f32[16,2048]{1,0:T(8,128)}, bf16[192,512]{1,0:T(8,128)(2,1)}, f32[768,512]{1,0:T(8,128)}, /*index=5*/f32[768,512]{1,0:T(8,128)}) custom-call(s32[16]{0:T(128)} %bitcast.173, s32[1]{0:T(128)} %bitcast.1.flags.flag, ...), custom_call_target="tpu_custom_call", output_to_operand_aliasing={{0}: (22, {})} | custom-call | bytes 42000000 | tf_op jit(solution)/shard_map/attend_backward/pallas_call | solution.py:423
  493.5 16.2 %ffn_weight_grads.5 = bf16[4,8,128,1024]{3,2,1,0:T(8,128)(2,1)} custom-call(s32[1]{0:T(128)} %bitcast.21.core, bf16[768,2048]{1,0:T(8,128)(2,1)} %get-tuple-element.285.g, bf16[768,2048]{1,0:T(8,128)(2,1)} %get-tuple-element.286.refs_0_, bf16[768,2048]{1,0:T(8,128)(2,1)} %get-tuple-element.287.refs_1_, bf16[8,512,1024]{2,1,0:T(8,128)(2,1)} %collective-permute-done.38.refs_2_), custom_call_target="tpu_custom_call" | custom-call | bytes 52500000 | tf_op jit(solution)/shard_map/ffn_weight_grads/pallas_call | solution.py:815
  514.7 12.5 %attend_backward.6 = (f32[768,2048]{1,0:T(8,128)}, bf16[192,2048]{1,0:T(8,128)(2,1)}, f32[16,2048]{1,0:T(8,128)}, bf16[192,512]{1,0:T(8,128)(2,1)}, f32[768,512]{1,0:T(8,128)}, /*index=5*/f32[768,512]{1,0:T(8,128)}) custom-call(s32[16]{0:T(128)} %bitcast.174, s32[1]{0:T(128)} %bitcast.1.flags.flag, ...), custom_call_target="tpu_custom_call", output_to_operand_aliasing={{0}: (22, {})} | custom-call | bytes 42000000 | tf_op jit(solution)/shard_map/attend_backward/pallas_call | solution.py:423
  532.6 12.7 %attend_backward.7 = (f32[768,2048]{1,0:T(8,128)}, bf16[192,2048]{1,0:T(8,128)(2,1)}, f32[16,2048]{1,0:T(8,128)}, bf16[192,512]{1,0:T(8,128)(2,1)}, bf16[768,512]{1,0:T(8,128)(2,1)}, /*index=5*/bf16[768,512]{1,0:T(8,128)(2,1)}) custom-call(s32[16]{0:T(128)} %bitcast.175, s32[1]{0:T(128)} %bitcast.1.flags.flag, ...), custom_call_target="tpu_custom_call", output_to_operand_aliasing={{0}: (22, {})} | custom-call | bytes 42000000 | tf_op jit(solution)/shard_map/attend_backward/pallas_call | solution.py:423
  591.5 27.1 %collective-permute-done.43 = bf16[2,2,128,1024]{3,2,1,0:T(8,128)(2,1)S(1)} collective-permute-done((bf16[2,2,128,1024]{3,2,1,0:T(8,128)(2,1)}, bf16[2,2,128,1024]{3,2,1,0:T(8,128)(2,1)S(1)}, u32[]{:S(2)}, u32[]{:S(2)}) %collective-permute-start.43) | collective-permute-done | bytes 1048608 | tf_op jit(solution)/shard_map/ppermute | solution.py:1269
  693.7 35.9 %update_blocks.2 = (f32[4,1024,1024]{2,1,0:T(8,128)}, f32[4,1024,1024]{2,1,0:T(8,128)}, f32[4,1024,1024]{2,1,0:T(8,128)}, f32[4,1024,1024]{2,1,0:T(8,128)}) custom-call(s32[8]{0:T(128)} %pad_add_fusion.4.begin, f32[3,4]{1,0:T(4,128)} %pad_maximum_fusion.7.factor, bf16[2,128,1024]{2,1,0:T(8,128)(2,1)} %get-tuple-element.348.refs_0_, ...), custom_call_target="tpu_custom_call" | custom-call | bytes 98000000 | tf_op jit(solution)/shard_map/update_blocks/pallas_call | solution.py:1089
  734.9 36.3 %update_blocks.3 = (f32[4,1024,1024]{2,1,0:T(8,128)}, f32[4,1024,1024]{2,1,0:T(8,128)}, f32[4,1024,1024]{2,1,0:T(8,128)}, f32[4,1024,1024]{2,1,0:T(8,128)}) custom-call(s32[8]{0:T(128)} %pad_add_fusion.4.begin, f32[3,4]{1,0:T(4,128)} %pad_maximum_fusion.7.factor, ...), custom_call_target="tpu_custom_call", output_to_operand_aliasing={{0}: (15, {}), {1}: (16, {}), {2}: (17, {}), {3}: (18, {})} | custom-call | bytes 98000000 | tf_op jit(solution)/shard_map/update_blocks/pallas_call | solution.py:1089
  (404 shorter events, 324.9 us)
Async XLA Ops:
  7.2 236.0 %all-gather.3.cloned.1.call-start = ((), (), s32[]{:S(2)}) async-start(), calls=%async_computation.4 | async-start | bytes 28311552 | tf_op jit(solution)/shard_map/all_gather | solution.py:1158
  12.7 32.7 %collective-permute-start.3 = (bf16[4,128,1024]{2,1,0:T(8,128)(2,1)}, bf16[4,128,1024]{2,1,0:T(8,128)(2,1)S(1)}, u32[]{:S(2)}, u32[]{:S(2)}) collective-permute-start(bf16[4,128,1024]{2,1,0:T(8,128)(2,1)} %get-tuple-element.386), channel_id=1, source_target_pairs={{0,4},{4,0},{8,12},{12,8},{1,5},{5,1},{9,13},{13,9},{2,6},{6,2},{1... | collective-permute-start | bytes 3145736 | tf_op jit(solution)/shard_map/ppermute | solution.py:1145
  15.7 46.1 %collective-permute-start.4 = (bf16[4,128,1024]{2,1,0:T(8,128)(2,1)S(1)}, bf16[4,128,1024]{2,1,0:T(8,128)(2,1)}, u32[]{:S(2)}, u32[]{:S(2)}) collective-permute-start(bf16[4,128,1024]{2,1,0:T(8,128)(2,1)S(1)} %get-tuple-element.388), channel_id=1, source_target_pairs={{0,8},{4,12},{8,0},{12,4},{1,9},{5,13},{9,1},{13,5},{2,10},{6,14},... | collective-permute-start | bytes 3145736 | tf_op jit(solution)/shard_map/ppermute | solution.py:1145
  17.2 45.7 %collective-permute-start.5 = (bf16[4,128,1024]{2,1,0:T(8,128)(2,1)S(1)}, bf16[4,128,1024]{2,1,0:T(8,128)(2,1)}, u32[]{:S(2)}, u32[]{:S(2)}) collective-permute-start(bf16[4,128,1024]{2,1,0:T(8,128)(2,1)S(1)} %get-tuple-element.385), channel_id=1, source_target_pairs={{0,12},{4,8},{8,4},{12,0},{1,13},{5,9},{9,5},{13,1},{2,14},{6,10},... | collective-permute-start | bytes 3145736 | tf_op jit(solution)/shard_map/ppermute | solution.py:1145
  67.5 464.2 %reduce-scatter.5.cloned.1.call-start = ((), (), s32[]{:S(2)}) async-start(), calls=%async_computation.2 | async-start | bytes 9437184 | tf_op jit(solution)/shard_map/reduce_scatter | solution.py:948
  83.1 47.2 %collective-permute-start.7 = (bf16[2,2,128,1024]{3,2,1,0:T(8,128)(2,1)S(1)}, bf16[2,2,128,1024]{3,2,1,0:T(8,128)(2,1)}, u32[]{:S(2)}, u32[]{:S(2)}) collective-permute-start(bf16[2,2,128,1024]{3,2,1,0:T(8,128)(2,1)S(1)} %pad_maximum_fusion.2), channel_id=1, source_target_pairs={{0,8},{4,12},{8,0},{12,4},{1,9},{5,13},{9,1},{13,5},{2,10},{6,14},... | collective-permute-start | bytes 3145736 | tf_op jit(solution)/shard_map/ppermute | solution.py:1165
  87.2 46.8 %collective-permute-start.10 = (bf16[2,2,128,1024]{3,2,1,0:T(8,128)(2,1)}, bf16[2,2,128,1024]{3,2,1,0:T(8,128)(2,1)}, u32[]{:S(2)}, u32[]{:S(2)}) collective-permute-start(bf16[2,2,128,1024]{3,2,1,0:T(8,128)(2,1)} %pad_maximum_fusion.3), channel_id=1, source_target_pairs={{0,4},{4,0},{8,12},{12,8},{1,5},{5,1},{9,13},{13,9},{2,6},{6,2},{1... | collective-permute-start | bytes 3145736 | tf_op jit(solution)/shard_map/ppermute | solution.py:1165
  88.1 54.7 %collective-permute-start = (f32[]{:T(128)}, f32[]{:T(128)}, u32[]{:S(2)}, u32[]{:S(2)}) collective-permute-start(f32[]{:T(128)} %convert_reduce_fusion), channel_id=1, source_target_pairs={{0,16},{16,0},{1,17},{17,1},{2,18},{18,2},{3,19},{19,3},{4,20},{20... | collective-permute-start | bytes 20 | tf_op jit(solution)/shard_map/ppermute | solution.py:100
  224.9 33.3 %collective-permute-start.16 = (bf16[192,2048]{1,0:T(8,128)(2,1)S(1)}, bf16[192,2048]{1,0:T(8,128)(2,1)S(1)}, u32[]{:S(2)}, u32[]{:S(2)}) collective-permute-start(bf16[192,2048]{1,0:T(8,128)(2,1)S(1)} %add_select_fusion.8.t_in.t1), channel_id=1, source_target_pairs={{0,1},{1,0},{2,3},{3,2},{4,5},{5,4},{6,7},{7,6},{8,9},{9,8},{10,11... | collective-permute-start | bytes 2359304 | tf_op jit(solution)/shard_map/ppermute | solution.py:147
  348.3 25.3 %collective-permute-start.26 = (bf16[192,2048]{1,0:T(8,128)(2,1)S(1)}, bf16[192,2048]{1,0:T(8,128)(2,1)}, u32[]{:S(2)}, u32[]{:S(2)}) collective-permute-start(bf16[192,2048]{1,0:T(8,128)(2,1)S(1)} %add.270), channel_id=1, source_target_pairs={{1,2},{2,1},{5,6},{6,5},{9,10},{10,9},{13,14},{14,13},{17,18},{18,... | collective-permute-start | bytes 2359304 | tf_op jit(solution)/shard_map/ppermute | solution.py:146
  351.4 24.7 %collective-permute-start.29 = (bf16[192,2048]{1,0:T(8,128)(2,1)S(1)}, bf16[192,2048]{1,0:T(8,128)(2,1)S(1)}, u32[]{:S(2)}, u32[]{:S(2)}) collective-permute-start(bf16[192,2048]{1,0:T(8,128)(2,1)S(1)} %add_select_fusion.3.t_in), channel_id=1, source_target_pairs={{0,1},{1,0},{2,3},{3,2},{4,5},{5,4},{6,7},{7,6},{8,9},{9,8},{10,11... | collective-permute-start | bytes 2359304 | tf_op jit(solution)/shard_map/ppermute | solution.py:147
  396.0 25.3 %collective-permute-start.31 = (bf16[192,2048]{1,0:T(8,128)(2,1)S(1)}, bf16[192,2048]{1,0:T(8,128)(2,1)S(1)}, u32[]{:S(2)}, u32[]{:S(2)}) collective-permute-start(bf16[192,2048]{1,0:T(8,128)(2,1)S(1)} %add.275), channel_id=1, source_target_pairs={{1,2},{2,1},{5,6},{6,5},{9,10},{10,9},{13,14},{14,13},{17,18},{18,... | collective-permute-start | bytes 2359304 | tf_op jit(solution)/shard_map/ppermute | solution.py:146
  398.2 25.4 %collective-permute-start.33 = (bf16[192,2048]{1,0:T(8,128)(2,1)S(1)}, bf16[192,2048]{1,0:T(8,128)(2,1)S(1)}, u32[]{:S(2)}, u32[]{:S(2)}) collective-permute-start(bf16[192,2048]{1,0:T(8,128)(2,1)S(1)} %add_select_fusion.1.t3), channel_id=1, source_target_pairs={{0,1},{1,0},{2,3},{3,2},{4,5},{5,4},{6,7},{7,6},{8,9},{9,8},{10,11... | collective-permute-start | bytes 2359304 | tf_op jit(solution)/shard_map/ppermute | solution.py:147
  436.2 189.2 %reduce-scatter.7.cloned.1.call-start = ((), (), s32[]{:S(2)}) async-start(), calls=%async_computation.5 | async-start | bytes 10485760
  437.3 28.9 %collective-permute-start.32 = (bf16[192,2048]{1,0:T(8,128)(2,1)S(1)}, bf16[192,2048]{1,0:T(8,128)(2,1)S(1)}, u32[]{:S(2)}, u32[]{:S(2)}) collective-permute-start(bf16[192,2048]{1,0:T(8,128)(2,1)S(1)} %copy-done.34), channel_id=1, source_target_pairs={{0,1},{1,0},{2,3},{3,2},{4,5},{5,4},{6,7},{7,6},{8,9},{9,8},{10,11... | collective-permute-start | bytes 2359304 | tf_op jit(solution)/shard_map/ppermute | solution.py:147
  437.3 29.1 %collective-permute-start.35 = (bf16[192,2048]{1,0:T(8,128)(2,1)S(1)}, bf16[192,2048]{1,0:T(8,128)(2,1)}, u32[]{:S(2)}, u32[]{:S(2)}) collective-permute-start(bf16[192,2048]{1,0:T(8,128)(2,1)S(1)} %add.277), channel_id=1, source_target_pairs={{1,2},{2,1},{5,6},{6,5},{9,10},{10,9},{13,14},{14,13},{17,18},{18,... | collective-permute-start | bytes 2359304 | tf_op jit(solution)/shard_map/ppermute | solution.py:146
  468.0 25.5 %collective-permute-start.38 = (bf16[8,512,1024]{2,1,0:T(8,128)(2,1)}, bf16[8,512,1024]{2,1,0:T(8,128)(2,1)}, u32[]{:S(2)}, u32[]{:S(2)}) collective-permute-start(bf16[8,512,1024]{2,1,0:T(8,128)(2,1)} %ffn_weight_grads.4), channel_id=1, source_target_pairs={{0,16},{16,0},{1,17},{17,1},{2,18},{18,2},{3,19},{19,3},{4,20},{20... | collective-permute-start | bytes 25165832 | tf_op jit(solution)/shard_map/ppermute | solution.py:937
  469.0 24.5 %collective-permute-start.36 = (bf16[192,2048]{1,0:T(8,128)(2,1)S(1)}, bf16[192,2048]{1,0:T(8,128)(2,1)}, u32[]{:S(2)}, u32[]{:S(2)}) collective-permute-start(bf16[192,2048]{1,0:T(8,128)(2,1)S(1)} %add.279.t3), channel_id=1, source_target_pairs={{0,1},{1,0},{2,3},{3,2},{4,5},{5,4},{6,7},{7,6},{8,9},{9,8},{10,11... | collective-permute-start | bytes 2359304 | tf_op jit(solution)/shard_map/ppermute | solution.py:147
  509.8 261.5 %all-reduce.3.cloned.1.call-start = ((), (), s32[]{:S(2)}) async-start(), calls=%async_computation.3 | async-start | bytes 6291456 | tf_op jit(solution)/shard_map/psum | solution.py:1275
  588.4 30.2 %collective-permute-start.43 = (bf16[2,2,128,1024]{3,2,1,0:T(8,128)(2,1)}, bf16[2,2,128,1024]{3,2,1,0:T(8,128)(2,1)S(1)}, u32[]{:S(2)}, u32[]{:S(2)}) collective-permute-start(bf16[2,2,128,1024]{3,2,1,0:T(8,128)(2,1)} %get-tuple-element.340), channel_id=1, source_target_pairs={{0,4},{4,0},{8,12},{12,8},{1,5},{5,1},{9,13},{13,9},{2,6},{6,2},{1... | collective-permute-start | bytes 3145736 | tf_op jit(solution)/shard_map/ppermute | solution.py:1269
  589.6 33.0 %collective-permute-start.45 = (bf16[2,2,128,1024]{3,2,1,0:T(8,128)(2,1)}, bf16[2,2,128,1024]{3,2,1,0:T(8,128)(2,1)S(1)}, u32[]{:S(2)}, u32[]{:S(2)}) collective-permute-start(bf16[2,2,128,1024]{3,2,1,0:T(8,128)(2,1)} %get-tuple-element.343), channel_id=1, source_target_pairs={{0,8},{4,12},{8,0},{12,4},{1,9},{5,13},{9,1},{13,5},{2,10},{6,14},... | collective-permute-start | bytes 3145736 | tf_op jit(solution)/shard_map/ppermute | solution.py:1269
  689.3 40.3 %collective-permute-start.60 = (bf16[2,128,1024]{2,1,0:T(8,128)(2,1)}, bf16[2,128,1024]{2,1,0:T(8,128)(2,1)S(1)}, u32[]{:S(2)}, u32[]{:S(2)}) collective-permute-start(bf16[2,128,1024]{2,1,0:T(8,128)(2,1)} %get-tuple-element.361), channel_id=1, source_target_pairs={{0,4},{4,0},{8,12},{12,8},{1,5},{5,1},{9,13},{13,9},{2,6},{6,2},{1... | collective-permute-start | bytes 1572872 | tf_op jit(solution)/shard_map/ppermute | solution.py:1304
  690.0 39.6 %collective-permute-start.61 = (bf16[2,128,1024]{2,1,0:T(8,128)(2,1)}, bf16[2,128,1024]{2,1,0:T(8,128)(2,1)}, u32[]{:S(2)}, u32[]{:S(2)}) collective-permute-start(bf16[2,128,1024]{2,1,0:T(8,128)(2,1)} %get-tuple-element.364), channel_id=1, source_target_pairs={{0,8},{4,12},{8,0},{12,4},{1,9},{5,13},{9,1},{13,5},{2,10},{6,14},... | collective-permute-start | bytes 1572872 | tf_op jit(solution)/shard_map/ppermute | solution.py:1304
  691.4 38.3 %collective-permute-start.62 = (bf16[2,128,1024]{2,1,0:T(8,128)(2,1)}, bf16[2,128,1024]{2,1,0:T(8,128)(2,1)}, u32[]{:S(2)}, u32[]{:S(2)}) collective-permute-start(bf16[2,128,1024]{2,1,0:T(8,128)(2,1)} %get-tuple-element.367), channel_id=1, source_target_pairs={{0,12},{4,8},{8,4},{12,0},{1,13},{5,9},{9,5},{13,1},{2,14},{6,10},... | collective-permute-start | bytes 1572872 | tf_op jit(solution)/shard_map/ppermute | solution.py:1304
  (126 other events, 1595.6 us)
Sparse Core Ops, SparseCore 0:
  67.6 148.5 all-gather.2
  436.3 70.3 reduce-scatter.4
  510.6 92.1 reduce-scatter.6
  625.6 121.0 all-reduce.2
